TPU v7x, 256 devices: a whole 4x4x8 slice. The times are simulated.
256 devices in a mesh: dp: 32 (over x_lo, z, core), tensor: 8 (over y, x_hi).
Axes of the slice: x: 4 (x_hi: 2, x_lo: 2; x = x_hi * 2 + x_lo), y: 4, z: 8, core: 2. Of those that a mesh axis runs over, the one named last changes fastest.
Arguments:
- clips: bfloat16 [32, 8, 8, 16, 1024], P('dp', None, None, None, 'tensor'), may hold values from -6 to 6
- out_grad: bfloat16 [32, 8, 8, 16, 1024], P('dp', None, None, None, 'tensor'), may hold values from -6 to 6
- spatial_weight: bfloat16 [3, 3, 1024, 1024], P(None, None, None, 'tensor'), may hold values from -0.0625 to 0.0625
- temporal_weight: bfloat16 [3, 1024, 1024], P(None, 'tensor'), may hold values from -0.109375 to 0.109375
Outputs:
- mixed: bfloat16 [32, 8, 8, 16, 1024], P('dp', None, None, None, 'tensor')
- clip_grad: bfloat16 [32, 8, 8, 16, 1024], P('dp', None, None, None, 'tensor')
- spatial_grad: bfloat16 [3, 3, 1024, 1024], P(None, None, 'dp', 'tensor')
- temporal_grad: bfloat16 [3, 1024, 1024], P(None, 'tensor', 'dp')
All inputs are finite; a program needn't handle non-finite values.
Results may differ from a plain program's by a relative error of at most 0.006.
Values may be sent and summed in bfloat16 or wider, within the bound.
No kernel may reach another device: no remote copies, remote signals or barrier semaphores. Data moves between devices by JAX's collectives and lax.ppermute only.
A program may use at most 128 MiB of HBM per device.

v0:
```python
import jax
import jax.numpy as jnp
from jax import lax
from jax.sharding import PartitionSpec as P

GS = 32


def group_silu(values):
    shaped = values.reshape(values.shape[0], -1, values.shape[-1] // GS, GS)
    center = jnp.mean(shaped, axis=(1, 3), keepdims=True)
    offsets = shaped - center
    spread = jnp.mean(offsets * offsets, axis=(1, 3), keepdims=True)
    return jax.nn.silu(offsets * lax.rsqrt(spread + 1e-05)).reshape(values.shape)


def spatial_conv(inputs, kernel):
    dims = inputs.shape
    flat = inputs.reshape((dims[0] * dims[1], dims[2], dims[3], dims[4]))
    result = lax.conv_general_dilated(
        flat,
        kernel,
        (1, 1),
        ((1, 1), (1, 1)),
        dimension_numbers=("NHWC", "HWIO", "NHWC"),
        preferred_element_type=jnp.float32,
    )
    return result.reshape(dims[:4] + (kernel.shape[3],))


def flipped(kernel):
    return jnp.transpose(kernel[::-1, ::-1], (0, 1, 3, 2))


def spatial_wgrad(inputs, grads):
    dims = inputs.shape
    padded = jnp.pad(inputs, ((0, 0), (0, 0), (1, 1), (1, 1), (0, 0)))
    right_side = grads.reshape(-1, grads.shape[-1])
    collected = []
    for row_tap in range(3):
        for col_tap in range(3):
            window = padded[:, :, row_tap : row_tap + dims[2], col_tap : col_tap + dims[3]].reshape(
                -1, dims[4]
            )
            collected.append(
                lax.dot_general(
                    window, right_side, (((0,), (0,)), ((), ())), preferred_element_type=jnp.float32
                )
            )
    return jnp.stack(collected).reshape(3, 3, dims[4], grads.shape[-1])


def temporal_conv(inputs, kernel):
    frame_count = inputs.shape[1]
    padded = jnp.pad(inputs, ((0, 0), (1, 1), (0, 0), (0, 0), (0, 0)))
    result = jnp.zeros((inputs.size // inputs.shape[-1], kernel.shape[2]), jnp.float32)
    for kernel_tap in range(3):
        window = padded[:, kernel_tap : kernel_tap + frame_count].reshape(-1, inputs.shape[-1])
        result = result + jnp.dot(window, kernel[kernel_tap], preferred_element_type=jnp.float32)
    return result.reshape(inputs.shape[:4] + (kernel.shape[2],))


def temporal_back(grads, kernel):
    frame_count = grads.shape[1]
    padded = jnp.pad(grads, ((0, 0), (1, 1), (0, 0), (0, 0), (0, 0)))
    result = jnp.zeros((grads.size // grads.shape[-1], kernel.shape[1]), jnp.float32)
    for kernel_tap in range(3):
        window = padded[:, 2 - kernel_tap : 2 - kernel_tap + frame_count].reshape(
            -1, grads.shape[-1]
        )
        result = result + lax.dot_general(
            window, kernel[kernel_tap], (((1,), (1,)), ((), ())), preferred_element_type=jnp.float32
        )
    return result.reshape(grads.shape[:4] + (kernel.shape[1],))


def temporal_wgrad(inputs, grads):
    frame_count = inputs.shape[1]
    padded = jnp.pad(inputs, ((0, 0), (1, 1), (0, 0), (0, 0), (0, 0)))
    right_side = grads.reshape(-1, grads.shape[-1])
    collected = []
    for kernel_tap in range(3):
        window = padded[:, kernel_tap : kernel_tap + frame_count].reshape(-1, inputs.shape[-1])
        collected.append(
            lax.dot_general(
                window, right_side, (((0,), (0,)), ((), ())), preferred_element_type=jnp.float32
            )
        )
    return jnp.stack(collected)


def per_device(clips, out_grad, spatial_weight, temporal_weight):
    position_count = (
        clips.shape[0] * clips.shape[1] * clips.shape[2] * clips.shape[3] * lax.axis_size("dp")
    )
    grad_scale = 1.0 / jnp.sqrt(jnp.float32(position_count))
    first_act, pull_first = jax.vjp(group_silu, clips.astype(jnp.float32))
    hidden_first = first_act.astype(jnp.bfloat16)
    first_full = lax.all_gather(hidden_first, "tensor", axis=4, tiled=True)
    spatial_out = spatial_conv(first_full, spatial_weight)
    second_act, pull_second = jax.vjp(group_silu, spatial_out)
    hidden_second = second_act.astype(jnp.bfloat16)
    temporal_out = lax.psum_scatter(
        temporal_conv(hidden_second, temporal_weight), "tensor", scatter_dimension=4, tiled=True
    )
    mixed = (clips.astype(jnp.float32) + temporal_out).astype(jnp.bfloat16)
    grad_full = lax.all_gather(out_grad, "tensor", axis=4, tiled=True)
    grad_second = temporal_back(grad_full, temporal_weight)
    grad_spatial = pull_second(grad_second)[0].astype(jnp.bfloat16)
    temporal_local = temporal_wgrad(hidden_second, grad_full)
    grad_partial = spatial_conv(grad_spatial, flipped(spatial_weight))
    grad_first = lax.psum_scatter(grad_partial, "tensor", scatter_dimension=4, tiled=True)
    spatial_local = spatial_wgrad(first_full, grad_spatial)
    spatial_share, temporal_share = (
        lax.psum_scatter(spatial_local, "dp", scatter_dimension=2, tiled=True),
        lax.psum_scatter(temporal_local, "dp", scatter_dimension=2, tiled=True),
    )
    clip_grad = (out_grad.astype(jnp.float32) + pull_first(grad_first)[0]).astype(jnp.bfloat16)
    spatial_out_grad = (spatial_share * grad_scale).astype(jnp.bfloat16)
    temporal_out_grad = (temporal_share * grad_scale).astype(jnp.bfloat16)
    return (mixed, clip_grad, spatial_out_grad, temporal_out_grad)


def solution(mesh):
    placed = (
        P("dp", None, None, None, "tensor"),
        P("dp", None, None, None, "tensor"),
        P(None, None, None, "tensor"),
        P(None, "tensor", None),
    )
    return jax.shard_map(
        per_device,
        mesh=mesh,
        in_specs=placed,
        out_specs=(
            P("dp", None, None, None, "tensor"),
            P("dp", None, None, None, "tensor"),
            P(None, None, "dp", "tensor"),
            P(None, "tensor", "dp"),
        ),
        check_vma=False,
    )
```

profile of v0, /device:TPU:14, one launch (start us, length us, event | category | flops | bytes accessed | tf_op | source)
XLA Modules:
  0.0 700.5 jit_solution(4739964253537896004)
XLA Ops:
  7.2 1.3 convert_reduce_fusion
  8.9 1.1 fusion.110
  10.4 1.9 fusion.107
  12.3 1.8 copy.86
  14.2 57.7 %all-gather.3.cloned.1.call-done = bf16[1,8,8,16,1024]{4,1,3,2,0:T(8,128)(2,1)} async-done(((bf16[1,8,8,16,128]{4,1,3,2,0:T(8,128)(2,1)}), bf16[1,8,8,16,1024]{4,1,3,2,0:T(8,128)(2,1)}) %all-gather.3.cloned.1.call-update) | async-done | bytes 2097168 | tf_op jit(solution)/shard_map/all_gather | solution.py:99
  72.0 6.6 fusion.151
  79.0 0.9 copy.93
  80.4 52.1 %all-gather.5.cloned.1.call-done = bf16[1,8,8,16,1024]{4,1,3,2,0:T(8,128)(2,1)} async-done(((bf16[1,8,8,16,128]{4,1,3,2,0:T(8,128)(2,1)}), bf16[1,8,8,16,1024]{4,1,3,2,0:T(8,128)(2,1)}) %all-gather.5.cloned.1.call-update) | async-done | bytes 2097168 | tf_op jit(solution)/shard_map/all_gather | solution.py:107
  132.5 3.4 pad_slice_fusion
  135.8 1.2 copy.90
  137.0 1.2 copy.88
  138.2 0.7 fusion.128
  138.9 0.9 copy-done.1
  139.8 1.2 copy.89
  140.9 0.7 convolution_add_fusion.1
  141.6 0.7 convolution_add_fusion
  143.2 1.5 fusion.120
  145.1 1.7 fusion.116
  146.7 2.1 fusion.40
  149.8 1.4 pad_maximum_fusion
  151.2 2.8 copy.94
  154.1 4.5 convolution_bitcast_fusion
  158.9 0.8 copy-done.6
  159.8 0.7 fusion.130
  160.5 0.7 fusion.126
  161.2 0.7 add_add_fusion
  161.9 4.4 copy.85
  166.6 3.3 fusion.94
  169.8 1.7 fusion.88
  171.5 1.7 fusion.82
  173.2 1.8 fusion.76
  175.0 1.7 fusion.37
  176.7 1.8 fusion.70
  178.5 1.7 fusion.64
  180.2 1.7 fusion.58
  181.9 1.7 fusion.52
  183.6 0.6 copy-done.9
  185.5 196.5 %all-reduce.6.cloned.1.call-done = f32[3,128,1024]{1,0,2:T(4,128)} async-done(((f32[3,128,1024]{1,0,2:T(4,128)}), f32[3,128,1024]{1,0,2:T(4,128)}) %all-reduce.6.cloned.1.call-update) | async-done | bytes 1572880
  382.0 0.9 fusion.139
  382.8 0.6 copy.97
  383.5 90.2 %reduce-scatter.6.cloned.1.call-done = f32[1,8,8,16,128]{4,1,3,2,0:T(8,128)} async-done(((f32[1,8,8,16,1024]{4,1,3,2,0:T(8,128)}), f32[1,8,8,16,128]{4,1,3,2,0:T(8,128)}) %reduce-scatter.6.cloned.1.call-update) | async-done | bytes 524304 | tf_op jit(solution)/shard_map/reduce_scatter | solution.py:112
  473.7 1.4 fusion.111
  476.0 90.2 %reduce-scatter.4.cloned.1.call-done = f32[1,8,8,16,128]{4,1,3,2,0:T(8,128)} async-done(((f32[1,8,8,16,1024]{4,1,3,2,0:T(8,128)}), f32[1,8,8,16,128]{4,1,3,2,0:T(8,128)}) %reduce-scatter.4.cloned.1.call-update) | async-done | bytes 524304 | tf_op jit(solution)/shard_map/reduce_scatter | solution.py:103
  566.2 1.4 add_convert_fusion
  567.6 0.7 copy.96
  568.4 0.7 copy.95
  569.1 122.9 %reduce-scatter.8.cloned.1.call-done = f32[3,3,32,128]{3,2,1,0:T(8,128)} async-done(((f32[3,3,1024,128]{3,2,1,0:T(8,128)}), f32[3,3,32,128]{3,2,1,0:T(8,128)}) %reduce-scatter.8.cloned.1.call-update) | async-done | bytes 147472 | tf_op jit(solution)/shard_map/reduce_scatter | solution.py:115
  692.1 1.6 multiply_convert_fusion.1
  (79 shorter events, 6.2 us)
Async XLA Ops:
  7.2 64.8 %copy-start = (bf16[3,3,1024,128]{3,2,1,0:T(8,128)(2,1)S(1)}, bf16[3,3,1024,128]{3,2,1,0:T(8,128)(2,1)}, u32[]{:S(2)}) copy-start(bf16[3,3,1024,128]{3,2,1,0:T(8,128)(2,1)} %param.6) | copy-start | bytes 7077892
  7.2 64.8 %all-gather.3.cloned.1.call-start = ((), (), s32[]{:S(2)}) async-start(), calls=%async_computation.3 | async-start | bytes 2359296 | tf_op jit(solution)/shard_map/all_gather | solution.py:99
  12.3 120.2 %all-gather.5.cloned.1.call-start = ((), (), s32[]{:S(2)}) async-start(), calls=%async_computation.5 | async-start | bytes 2359296 | tf_op jit(solution)/shard_map/all_gather | solution.py:107
  14.2 367.8 %all-reduce.6.cloned.1.call-start = ((), (), s32[]{:S(2)}) async-start(), calls=%async_computation.8 | async-start | bytes 4194304
  137.0 1.2 copy-start.5
  138.2 1.6 copy-start.1
  142.4 2.6 copy-start.4
  145.1 3.8 copy-start.2
  154.0 319.7 %reduce-scatter.6.cloned.1.call-start = ((), (), s32[]{:S(2)}) async-start(), calls=%async_computation.6 | async-start | bytes 4718592 | tf_op jit(solution)/shard_map/reduce_scatter | solution.py:112
  158.6 407.6 %reduce-scatter.4.cloned.1.call-start = ((), (), s32[]{:S(2)}) async-start(), calls=%async_computation.4 | async-start | bytes 4718592 | tf_op jit(solution)/shard_map/reduce_scatter | solution.py:103
  158.7 1.1 copy-start.6
  166.3 525.8 %reduce-scatter.8.cloned.1.call-start = ((), (), s32[]{:S(2)}) async-start(), calls=%async_computation.7 | async-start | bytes 4866048 | tf_op jit(solution)/shard_map/reduce_scatter | solution.py:115
  166.5 3.3 copy-start.8
  183.6 0.7 copy-start.9
  183.6 290.1 %copy-start.3 = (bf16[1,8,8,16,128]{4,3,2,1,0:T(8,128)(2,1)S(1)}, bf16[1,8,8,16,128]{4,3,2,1,0:T(8,128)(2,1)}, u32[]{:S(2)}) copy-start(bf16[1,8,8,16,128]{4,3,2,1,0:T(8,128)(2,1)} %param.4) | copy-start | bytes 786436
  183.6 382.6 %copy-start.7 = (bf16[1,8,8,16,128]{4,3,2,1,0:T(8,128)(2,1)S(1)}, bf16[1,8,8,16,128]{4,3,2,1,0:T(8,128)(2,1)}, u32[]{:S(2)}) copy-start(bf16[1,8,8,16,128]{4,3,2,1,0:T(8,128)(2,1)} %param.5) | copy-start | bytes 786436
Sparse Core Ops, SparseCore 0:
  12.4 59.5 all-gather.2
  75.0 57.4 all-gather.4
  154.1 227.8 all-reduce.5
  386.5 87.1 reduce-scatter.5
  477.6 88.5 reduce-scatter.3
  568.8 123.2 reduce-scatter.7
where the time goes:
time: 702 us; the launch traced here: 700 us
  waiting for transfers between devices  610 us (87%)
  matrix products  35.4 us (5%)
  local copies, waits for them, and re-layouts  24 us (3%)
  other arithmetic  15.9 us (2%)
  between operations  15 us (2%)
    unnamed x7, waiting for transfers between devices  197 us
    reduce_scatter x1, waiting for transfers between devices, per_device(): lax.psum_scatter(spatial_local, 'dp', scatter_dimension=2, tiled=True)  123 us
    reduce_scatter x1, waiting for transfers between devices, per_device(): lax.psum_scatter(grad_partial, 'tensor', scatter_dimension=4, tiled=True)  90.2 us
    reduce_scatter x1, waiting for transfers between devices, per_device(): lax.psum_scatter(temporal_conv(hidden_second, temporal_weight), 'tensor',...  90.2 us
    all_gather x1, waiting for transfers between devices, per_device(): first_full = lax.all_gather(hidden_first, 'tensor', axis=4, tiled=True)  57.7 us
    all_gather x1, waiting for transfers between devices, per_device(): grad_full = lax.all_gather(out_grad, 'tensor', axis=4, tiled=True)  52.1 us
    dot_general x9, matrix products, spatial_wgrad(): lax.dot_general(window, right_side, (((0,), (0,)), ((), ())), preferred_e...  17 us
  transfers between devices with their start and end apart: 6, of which 6 were waited for; matrix products, arithmetic and copies ran while one was open for 7% of the time, Pallas kernels for 0%

commit v1 on v0

v1 whole, which is shorter than its diff:
```python
import jax
import jax.numpy as jnp
from jax import lax
from jax.sharding import PartitionSpec as P

GS = 32
BF = jnp.bfloat16
F32 = jnp.float32
Y_GROUPS = [[y * 2 + h for y in range(4)] for h in range(2)]
X_GROUPS = [[2 * y, 2 * y + 1] for y in range(4)]
CORE_GROUPS = [[2 * k, 2 * k + 1] for k in range(16)]
XLO_GROUPS = [[k, k + 16] for k in range(16)]
Z_GROUPS = [[l * 16 + z * 2 + c for z in range(8)] for l in range(2) for c in range(2)]


def swap(values, axis, groups):
    return lax.all_to_all(
        values, axis, split_axis=0, concat_axis=0, tiled=True, axis_index_groups=groups
    )


def over_y(values):
    return swap(values, "tensor", Y_GROUPS)


def over_x(values):
    return swap(values, "tensor", X_GROUPS)


def group_mean(values):
    lanes = jnp.sum(values, axis=0).reshape(-1, GS)
    means = jnp.sum(lanes, axis=1, keepdims=True) / (values.shape[0] * GS)
    return jnp.broadcast_to(means, lanes.shape).reshape(1, -1)


def normalize(values):
    offsets = values - group_mean(values)
    scale = lax.rsqrt(group_mean(offsets * offsets) + 1e-05)
    return offsets * scale, scale


def act(unit):
    return unit * jax.nn.sigmoid(unit)


def act_back(unit, scale, grads):
    gate = jax.nn.sigmoid(unit)
    inner = grads * (gate * (1.0 + unit * (1.0 - gate)))
    return scale * (inner - group_mean(inner) - unit * group_mean(inner * unit))


def conv(inputs, kernel):
    return lax.conv_general_dilated(
        inputs.reshape(8, 8, 16, -1),
        kernel,
        (1, 1),
        ((1, 1), (1, 1)),
        dimension_numbers=("NHWC", "HWIO", "NHWC"),
        preferred_element_type=F32,
    ).reshape(1024, -1)


def shifts(values):
    padded = jnp.pad(values.reshape(8, 8, 16, -1), ((0, 0), (1, 1), (1, 1), (0, 0)))
    return [
        padded[:, a : a + 8, b : b + 16].reshape(1024, -1) for a in (2, 1, 0) for b in (2, 1, 0)
    ]


def frame_shifts(values):
    padded = jnp.pad(values, ((128, 128), (0, 0)))
    return [padded[128 * k : 128 * k + 1024] for k in range(3)]


def tdot(left, right):
    return lax.dot_general(left, right, (((0,), (0,)), ((), ())), preferred_element_type=F32)


def wide(parts):
    return jnp.concatenate(list(parts), axis=1)


def per_device(clips, out_grad, spatial_weight, temporal_weight):
    tensor, data = lax.axis_index("tensor"), lax.axis_index("dp")
    x_hi, core = tensor % 2, data % 2
    z_mid = (data // 4) % 2
    grad_scale = 1.0 / jnp.sqrt(jnp.float32(32768))
    grads = out_grad.reshape(1024, 128)
    grads_all = over_y(jnp.broadcast_to(grads, (4, 1024, 128)).reshape(4096, 128))
    grads_all = wide(grads_all.reshape(4, 1024, 128))

    spatial_split = spatial_weight.reshape(9, 4, 2, 128, 128)
    temporal_split = temporal_weight.reshape(3, 128, 4, 2, 128)
    spatial_keep = lax.dynamic_index_in_dim(spatial_split, x_hi, 2, False)
    temporal_keep = lax.dynamic_index_in_dim(temporal_split, x_hi, 3, False)
    spatial_give = lax.dynamic_index_in_dim(spatial_split, 1 - x_hi, 2, False)
    temporal_give = lax.dynamic_index_in_dim(temporal_split, 1 - x_hi, 3, False)
    spatial_give = lax.dynamic_slice_in_dim(spatial_give, 2 * core, 2, 1)
    temporal_give = lax.dynamic_slice_in_dim(temporal_give, 2 * core, 2, 2)
    temporal_give = jnp.moveaxis(temporal_give, 2, 1)
    packed = jnp.concatenate([spatial_give.reshape(-1, 128), temporal_give.reshape(-1, 128)])
    cross = []
    for d in range(32):
        for t in range(8):
            cross.append((d * 8 + t, ((d + 16) % 32) * 8 + (t ^ 1)))
    packed = lax.ppermute(packed, ("dp", "tensor"), cross)
    rows = packed.shape[0]
    packed = swap(jnp.broadcast_to(packed, (2, rows, 128)).reshape(-1, 128), "dp", CORE_GROUPS)
    packed = packed.reshape(2, rows, 128)
    spatial_got = packed[:, : 9 * 256].reshape(2, 9, 2, 128, 128)
    spatial_got = jnp.moveaxis(spatial_got, 0, 1).reshape(9, 512, 128)
    temporal_got = packed[:, 9 * 256 :].reshape(2, 3, 2, 128, 128)
    temporal_got = jnp.moveaxis(temporal_got, (0, 1, 2, 3, 4), (2, 0, 3, 1, 4)).reshape(3, 128, 512)
    first = x_hi == 0
    spatial_keep = spatial_keep.reshape(9, 512, 128)
    temporal_keep = temporal_keep.reshape(3, 128, 512)
    spatial = jnp.concatenate(
        [jnp.where(first, spatial_keep, spatial_got), jnp.where(first, spatial_got, spatial_keep)], 2
    )
    temporal = jnp.concatenate(
        [
            jnp.where(first, temporal_keep, temporal_got),
            jnp.where(first, temporal_got, temporal_keep),
        ],
        1,
    )

    clip_rows = clips.reshape(1024, 128).astype(F32)
    unit_first, scale_first = normalize(clip_rows)
    hidden_first = act(unit_first).astype(BF)
    first_all = over_y(jnp.broadcast_to(hidden_first, (4, 1024, 128)).reshape(4096, 128))
    first_all = wide(first_all.reshape(4, 1024, 128))

    second_part = sum(
        lax.dot_general(w, temporal[2 - k], (((1,), (1,)), ((), ())), preferred_element_type=F32)
        for k, w in enumerate(frame_shifts(grads_all))
    )
    second_part = second_part.astype(BF).reshape(1024, 2, 128).swapaxes(0, 1)
    second_part = over_x(second_part.reshape(2048, 128)).reshape(2, 1024, 128)
    grad_second = second_part[0].astype(F32) + second_part[1].astype(F32)

    spatial_part = conv(first_all, spatial.reshape(3, 3, 512, 256))
    spatial_part = spatial_part.astype(BF).reshape(1024, 2, 128).swapaxes(0, 1)
    spatial_part = over_x(spatial_part.reshape(2048, 128)).reshape(2, 1024, 128)
    spatial_out = spatial_part[0].astype(F32) + spatial_part[1].astype(F32)

    unit_second, scale_second = normalize(spatial_out)
    hidden_second = act(unit_second).astype(BF)
    grad_spatial = act_back(unit_second, scale_second, grad_second).astype(BF)
    both = jnp.stack([hidden_second, grad_spatial])
    both = over_x(jnp.broadcast_to(both, (2, 2, 1024, 128)).reshape(-1, 128))
    both = both.reshape(2, 2, 1024, 128)
    second_all = wide(both[:, 0])
    spatial_grads = wide(both[:, 1])

    shifted = jnp.concatenate(shifts(spatial_grads), axis=1)
    shifted_second = jnp.concatenate(frame_shifts(second_all), axis=1)
    spatial_local = tdot(first_all, shifted)
    temporal_local = tdot(grads_all, shifted_second)
    local = jnp.concatenate([spatial_local, temporal_local], axis=1)
    local = local.astype(BF).reshape(2, 2, 2, 2, 32, 12, 2, 128)
    local = local.transpose(3, 0, 1, 6, 2, 5, 4, 7)
    local = swap(local.reshape(-1, 128), "dp", CORE_GROUPS).reshape(2, -1, 128)
    local = (local[0].astype(F32) + local[1].astype(F32)).astype(BF)
    local = swap(local, "dp", XLO_GROUPS).reshape(2, -1, 128)
    local = (local[0].astype(F32) + local[1].astype(F32)).astype(BF)
    local = swap(local, "dp", Z_GROUPS).reshape(8, 12 * 32, 128)
    share = (jnp.sum(local.astype(F32), axis=0) * grad_scale).astype(BF)
    move = []
    for d in range(32):
        for t in range(8):
            if (d // 4) % 2 != t % 2:
                move.append((d * 8 + t, (d ^ 4) * 8 + (t ^ 1)))
    moved = lax.ppermute(share, ("dp", "tensor"), move)
    share = jnp.where(z_mid == x_hi, share, moved).reshape(12, 32, 128)
    spatial_share = share[:9].reshape(3, 3, 32, 128)
    temporal_share = share[9:].swapaxes(1, 2)

    temporal_part = sum(
        jnp.dot(w, temporal[k], preferred_element_type=F32)
        for k, w in enumerate(frame_shifts(second_all))
    )
    temporal_part = temporal_part.astype(BF).reshape(1024, 4, 128).swapaxes(0, 1)
    temporal_part = over_y(temporal_part.reshape(4096, 128)).reshape(4, 1024, 128)
    mixed = (clip_rows + jnp.sum(temporal_part.astype(F32), axis=0)).astype(BF)

    first_part = lax.dot_general(
        shifted,
        spatial.swapaxes(1, 2).reshape(9 * 256, 512),
        (((1,), (0,)), ((), ())),
        preferred_element_type=F32,
    )
    first_part = first_part.astype(BF).reshape(1024, 4, 128).swapaxes(0, 1)
    first_part = over_y(first_part.reshape(4096, 128)).reshape(4, 1024, 128)
    grad_first = jnp.sum(first_part.astype(F32), axis=0)
    clip_grad = (grads.astype(F32) + act_back(unit_first, scale_first, grad_first)).astype(BF)
    return (
        mixed.reshape(clips.shape),
        clip_grad.reshape(clips.shape),
        spatial_share,
        temporal_share,
    )


def solution(mesh):
    placed = (
        P("dp", None, None, None, "tensor"),
        P("dp", None, None, None, "tensor"),
        P(None, None, None, "tensor"),
        P(None, "tensor", None),
    )
    return jax.shard_map(
        per_device,
        mesh=mesh,
        in_specs=placed,
        out_specs=(
            P("dp", None, None, None, "tensor"),
            P("dp", None, None, None, "tensor"),
            P(None, None, "dp", "tensor"),
            P(None, "tensor", "dp"),
        ),
        check_vma=False,
    )
```

time: 702 us -> 272 us (0.39)
  waiting for transfers between devices: 610 us -> 95.8 us
  starting transfers between devices: 0.47 us -> 63.2 us
  local copies, waits for them, and re-layouts: 24 us -> 51.8 us
  between operations: 15 us -> 1.25 us
  matrix products: 35.4 us -> 25.5 us
  other arithmetic: 15.9 us -> 24.6 us
    reduce_scatter x3 -> x0, waiting for transfers between devices: 303 us -> none  [the longest x1 123 us: per_device(): lax.psum_scatter(spatial_local, 'dp', scatter_dimension=2, tiled=True)]
    unnamed x7 -> x0, waiting for transfers between devices: 197 us -> none
    all_gather x2 -> x0, waiting for transfers between devices: 110 us -> none  [the longest x1 57.7 us: per_device(): first_full = lax.all_gather(hidden_first, 'tensor', axis=4, tiled=True)]
    all_to_all x0 -> x10, waiting for transfers between devices: none -> 71.4 us  [swap(): lax.all_to_all(values, axis, split_axis=0, concat_axis=0, tiled=True, axi...]
    all_to_all x0 -> x10, starting transfers between devices: none -> 58.7 us  [swap(): lax.all_to_all(values, axis, split_axis=0, concat_axis=0, tiled=True, axi...]
    ppermute x0 -> x2, waiting for transfers between devices: none -> 24.3 us  [the longest x1 19.8 us: per_device(): packed = lax.ppermute(packed, ('dp', 'tensor'), cross)]
    convert_element_type x1 -> x4, local copies, waits for them, and re-layouts: 0.04 us -> 13.8 us  [the longest x2 12.8 us: per_device(): local = local.astype(BF).reshape(2, 2, 2, 2, 32, 12, 2, 128)]
    conv_general_dilated x2 -> x1, matrix products: 11.1 us -> 2.62 us  [conv(): lax.conv_general_dilated(inputs.reshape(8, 8, 16, -1), kernel, (1, 1), ((...]
  transfers between devices with their start and end apart: 6 -> 12, of which waited for: 6 -> 10; matrix products, arithmetic and copies ran while one was open for 7% -> 17% of each run, Pallas kernels for 0% -> 0%
where the time goes in v1:
time: 272 us; the launch traced here: 268 us
  waiting for transfers between devices  95.8 us (35%)
  starting transfers between devices  63.2 us (23%)
  local copies, waits for them, and re-layouts  51.8 us (19%)
  matrix products  25.5 us (9%)
  other arithmetic  24.6 us (9%)
  blocking collectives  5.97 us (2%)
    all_to_all x10, waiting for transfers between devices, swap(): lax.all_to_all(values, axis, split_axis=0, concat_axis=0, tiled=True, axi...  71.4 us
    all_to_all x10, starting transfers between devices, swap(): lax.all_to_all(values, axis, split_axis=0, concat_axis=0, tiled=True, axi...  58.7 us
    ppermute x1, waiting for transfers between devices, per_device(): packed = lax.ppermute(packed, ('dp', 'tensor'), cross)  19.8 us
    convert_element_type x2, local copies, waits for them, and re-layouts, per_device(): local = local.astype(BF).reshape(2, 2, 2, 2, 32, 12, 2, 128)  12.8 us
    dot_general x3, matrix products, per_device(): jnp.dot(w, temporal[k], preferred_element_type=F32)  7.33 us
    unnamed x64, local copies, waits for them, and re-layouts  6.99 us
    dot_general x1, matrix products, per_device(): lax.dot_general(shifted, spatial.swapaxes(1, 2).reshape(9 * 256, 512), ((...  6.76 us
    convert_element_type x2, other arithmetic, per_device(): local = (local[0].astype(F32) + local[1].astype(F32)).astype(BF)  6.08 us
  transfers between devices with their start and end apart: 12, of which 10 were waited for; matrix products, arithmetic and copies ran while one was open for 17% of the time, Pallas kernels for 0%

profile of v1, /device:TPU:14, one launch (start us, length us, event | category | flops | bytes accessed | tf_op | source)
XLA Modules:
  0.0 268.0 jit_solution(4593218936715131654)
XLA Ops:
  0.7 1.7 copy.61
  4.1 1.7 copy.62
  5.9 2.1 pad_maximum_fusion.2
  9.0 19.8 %collective-permute-done = bf16[3072,128]{1,0:T(8,128)(2,1)} collective-permute-done((bf16[3072,128]{1,0:T(8,128)(2,1)}, bf16[3072,128]{1,0:T(8,128)(2,1)}, u32[]{:S(2)}, u32[]{:S(2)}) %collective-permute-start) | collective-permute-done | bytes 786464 | tf_op jit(solution)/shard_map/ppermute | solution.py:106
  30.1 6.0 %all_to_all.69 = bf16[2,3072,128]{2,1,0:T(8,128)(2,1)} all-to-all(bf16[2,3072,128]{2,1,0:T(8,128)(2,1)S(1)} %broadcast_in_dim.29), channel_id=1, replica_groups={{0,8},{16,24},{32,40},{48,56},{64,72},{80,88},{96,104},{112,120},{128,1..., dimensions={0} | all-to-all | bytes 3145728 | tf_op jit(solution)/shard_map/all_to_all | solution.py:17
  37.2 4.9 %all-to-all-start.3 = ((bf16[4,1024,128]{2,1,0:T(8,128)(2,1)}), bf16[4,1024,128]{2,1,0:T(8,128)(2,1)}, u32[]{:S(2)}, u32[]{:S(2)}) async-start(bf16[4,1024,128]{2,1,0:T(8,128)(2,1)} %broadcast_in_dim.32), calls=%async_computation.3 | async-start | bytes 2097152 | tf_op jit(solution)/shard_map/all_to_all | solution.py:17
  46.7 9.6 %all-to-all-done.3 = bf16[4,1024,128]{2,1,0:T(8,128)(2,1)} async-done(((bf16[4,1024,128]{2,1,0:T(8,128)(2,1)}), bf16[4,1024,128]{2,1,0:T(8,128)(2,1)}, u32[]{:S(2)}, u32[]{:S(2)}) %all-to-all-start.3) | async-done | bytes 1048608 | tf_op jit(solution)/shard_map/all_to_all | solution.py:17
  57.4 5.6 %all-to-all-start = ((bf16[4,1024,128]{2,1,0:T(8,128)(2,1)}), bf16[4,1024,128]{2,1,0:T(8,128)(2,1)}, u32[]{:S(2)}, u32[]{:S(2)}) async-start(bf16[4,1024,128]{2,1,0:T(8,128)(2,1)} %broadcast_in_dim.28), calls=%async_computation | async-start | bytes 2097152 | tf_op jit(solution)/shard_map/all_to_all | solution.py:17
  65.7 1.5 convolution_add_fusion.1
  67.1 9.0 %all-to-all-done = bf16[4,1024,128]{2,1,0:T(8,128)(2,1)} async-done(((bf16[4,1024,128]{2,1,0:T(8,128)(2,1)}), bf16[4,1024,128]{2,1,0:T(8,128)(2,1)}, u32[]{:S(2)}, u32[]{:S(2)}) %all-to-all-start) | async-done | bytes 1048608 | tf_op jit(solution)/shard_map/all_to_all | solution.py:17
  76.2 2.3 slice_bitcast_fusion.9
  79.4 2.6 fusion.19
  83.1 1.9 copy.65
  85.0 4.8 %all-to-all-start.2 = ((bf16[2,1024,128]{2,1,0:T(8,128)(2,1)}), bf16[2,1024,128]{2,1,0:T(8,128)(2,1)S(1)}, u32[]{:S(2)}, u32[]{:S(2)}) async-start(bf16[2,1024,128]{2,1,0:T(8,128)(2,1)} %copy.65), calls=%async_computation.2 | async-start | bytes 1048576 | tf_op jit(solution)/shard_map/all_to_all | solution.py:17
  89.8 2.5 fusion.18
  92.3 2.0 copy.67
  94.3 7.0 %all-to-all-start.4 = ((bf16[2,1024,128]{2,1,0:T(8,128)(2,1)}), bf16[2,1024,128]{2,1,0:T(8,128)(2,1)S(1)}, u32[]{:S(2)}, u32[]{:S(2)}) async-start(bf16[2,1024,128]{2,1,0:T(8,128)(2,1)} %bitcast.30), calls=%async_computation.4 | async-start | bytes 1048576 | tf_op jit(solution)/shard_map/all_to_all | solution.py:17
  102.4 3.5 %all-to-all-done.4 = bf16[2,1024,128]{2,1,0:T(8,128)(2,1)S(1)} async-done(((bf16[2,1024,128]{2,1,0:T(8,128)(2,1)}), bf16[2,1024,128]{2,1,0:T(8,128)(2,1)S(1)}, u32[]{:S(2)}, u32[]{:S(2)}) %all-to-all-start.4) | async-done | bytes 524320 | tf_op jit(solution)/shard_map/all_to_all | solution.py:17
  110.2 7.9 %all-to-all-start.5 = ((bf16[2,2048,128]{2,1,0:T(8,128)(2,1)}), bf16[2,2048,128]{2,1,0:T(8,128)(2,1)}, u32[]{:S(2)}, u32[]{:S(2)}) async-start(bf16[2,2048,128]{2,1,0:T(8,128)(2,1)} %broadcast_in_dim.72), calls=%async_computation.5 | async-start | bytes 2097152 | tf_op jit(solution)/shard_map/all_to_all | solution.py:17
  118.2 1.7 bitcast_select_fusion.1
  119.9 6.4 %all-to-all-done.5 = bf16[2,2048,128]{2,1,0:T(8,128)(2,1)} async-done(((bf16[2,2048,128]{2,1,0:T(8,128)(2,1)}), bf16[2,2048,128]{2,1,0:T(8,128)(2,1)}, u32[]{:S(2)}, u32[]{:S(2)}) %all-to-all-start.5) | async-done | bytes 1048608 | tf_op jit(solution)/shard_map/all_to_all | solution.py:17
  127.6 1.8 fusion.60
  129.5 1.8 fusion.55
  136.1 2.1 copy-done.26
  138.3 3.3 %convolution_convert_fusion = bf16[512,2304]{1,0:T(8,128)(2,1)S(1)} fusion(bf16[1024,2304]{1,0:T(8,128)(2,1)S(1)} %constant_dynamic-update-slice_fusion, bf16[1024,128]{1,0:T(8,128)(2,1)S(1)} %copy-done.25, bf16[1024,128]{1,0:T(8,128)(2,1)S(1)} %copy-done.24, bf16[1024,128]{1,0:T(8,128)(2,1)S(1)} %copy-done.23, bf16[1024,128]{1,0:T(8,128)(2,1)S(1)} %copy-done.22), kind=kOutput, calls=%fused_computation | convolution fusion | flops 2421293056 | bytes 8126464 | tf_op jit(solution)/shard_map/dot_general | solution.py:76
  141.5 2.2 pad_maximum_fusion
  143.7 8.3 %convert_element_type.153 = bf16[2,2,2,2,32,12,2,128]{7,6,5,4,3,2,1,0:T(2,128)(2,1)} reshape(bf16[512,3072]{1,0:T(8,128)(2,1)} %pad_maximum_fusion) | data formatting | bytes 6291456 | tf_op jit(solution)/shard_map/convert_element_type | solution.py:161
  152.0 4.5 %copy.72 = bf16[2,2,2,2,32,12,2,128]{7,4,5,2,6,1,0,3:T(8,128)(2,1)} copy(bf16[2,2,2,2,32,12,2,128]{7,6,5,4,3,2,1,0:T(2,128)(2,1)} %convert_element_type.153) | data formatting | bytes 6291456 | tf_op jit(solution)/shard_map/convert_element_type | solution.py:161
  156.5 5.2 %all-to-all-start.8 = ((bf16[2,6144,128]{2,1,0:T(8,128)(2,1)}), bf16[2,6144,128]{2,1,0:T(8,128)(2,1)}, u32[]{:S(2)}, u32[]{:S(2)}) async-start(bf16[2,6144,128]{2,1,0:T(8,128)(2,1)} %bitcast.133), calls=%async_computation.8 | async-start | bytes 6291456 | tf_op jit(solution)/shard_map/all_to_all | solution.py:17
  161.7 3.7 %add_convert_fusion.1 = bf16[1024,512]{0,1:T(8,128)(2,1)} fusion(f32[1024,512]{0,1:T(8,128)} %fusion.55, f32[1024,512]{0,1:T(8,128)} %fusion.60, bf16[1024,256]{1,0:T(8,128)(2,1)S(1)} %pad_maximum_fusion.4, bf16[3,128,512]{1,2,0:T(8,128)(2,1)S(1)} %get-tuple-element.37, bf16[3,128,512]{1,2,0:T(8,128)(2,1)S(1)} %get-tuple-element.38), kind=kOutput, calls=%fused_computation.14 | convolution fusion | flops 270532608 | bytes 6553600 | tf_op jit(solution)/shard_map/dot_general | solution.py:180
  165.4 4.9 %all-to-all-start.6 = ((bf16[4,1024,128]{1,2,0:T(8,128)(2,1)}), bf16[4,1024,128]{1,2,0:T(8,128)(2,1)S(1)}, u32[]{:S(2)}, u32[]{:S(2)}) async-start(bf16[4,1024,128]{1,2,0:T(8,128)(2,1)} %bitcast.37), calls=%async_computation.6 | async-start | bytes 2097152 | tf_op jit(solution)/shard_map/all_to_all | solution.py:17
  170.4 3.5 %add_convert_fusion = bf16[1,6144,128]{2,1,0:T(8,128)(2,1)} fusion(bf16[2,6144,128]{2,1,0:T(8,128)(2,1)} %all-to-all-done.8), kind=kLoop, calls=%fused_computation.2 | loop fusion | flops 3145728 | bytes 4718592 | tf_op jit(solution)/shard_map/convert_element_type | solution.py:164
  173.9 11.0 %all-to-all-done.6 = bf16[4,1024,128]{1,2,0:T(8,128)(2,1)S(1)} async-done(((bf16[4,1024,128]{1,2,0:T(8,128)(2,1)}), bf16[4,1024,128]{1,2,0:T(8,128)(2,1)S(1)}, u32[]{:S(2)}, u32[]{:S(2)}) %all-to-all-start.6) | async-done | bytes 1048608 | tf_op jit(solution)/shard_map/all_to_all | solution.py:17
  184.9 4.9 %all-to-all-start.9 = ((bf16[2,3072,128]{2,1,0:T(8,128)(2,1)}), bf16[2,3072,128]{2,1,0:T(8,128)(2,1)}, u32[]{:S(2)}, u32[]{:S(2)}) async-start(bf16[2,3072,128]{2,1,0:T(8,128)(2,1)} %bitcast.65), calls=%async_computation.9 | async-start | bytes 3145728 | tf_op jit(solution)/shard_map/all_to_all | solution.py:17
  189.8 1.5 maximum_bitcast_fusion
  191.4 2.5 copy.70
  193.9 6.8 %convolution_convert_fusion.1 = bf16[1024,512]{0,1:T(8,128)(2,1)} fusion(bf16[1024,2304]{1,0:T(8,128)(2,1)} %copy-done.26, bf16[2304,512]{1,0:T(8,128)(2,1)} %bitcast.141), kind=kOutput, calls=%fused_computation.28 | convolution fusion | flops 2416443392 | bytes 8126464 | tf_op jit(solution)/shard_map/dot_general | solution.py:187
  200.6 7.0 %all-to-all-done.9 = bf16[2,3072,128]{2,1,0:T(8,128)(2,1)} async-done(((bf16[2,3072,128]{2,1,0:T(8,128)(2,1)}), bf16[2,3072,128]{2,1,0:T(8,128)(2,1)}, u32[]{:S(2)}, u32[]{:S(2)}) %all-to-all-start.9) | async-done | bytes 1572896 | tf_op jit(solution)/shard_map/all_to_all | solution.py:17
  207.6 4.9 %all-to-all-start.7 = ((bf16[4,1024,128]{1,2,0:T(8,128)(2,1)}), bf16[4,1024,128]{1,2,0:T(8,128)(2,1)S(1)}, u32[]{:S(2)}, u32[]{:S(2)}) async-start(bf16[4,1024,128]{1,2,0:T(8,128)(2,1)} %bitcast.57), calls=%async_computation.7 | async-start | bytes 2097152 | tf_op jit(solution)/shard_map/all_to_all | solution.py:17
  212.6 2.5 add_convert_fusion.2
  215.1 10.6 %all-to-all-done.7 = bf16[4,1024,128]{1,2,0:T(8,128)(2,1)S(1)} async-done(((bf16[4,1024,128]{1,2,0:T(8,128)(2,1)}), bf16[4,1024,128]{1,2,0:T(8,128)(2,1)S(1)}, u32[]{:S(2)}, u32[]{:S(2)}) %all-to-all-start.7) | async-done | bytes 1048608 | tf_op jit(solution)/shard_map/all_to_all | solution.py:17
  225.8 8.5 %all-to-all-start.10 = ((bf16[8,384,128]{2,1,0:T(8,128)(2,1)}), bf16[8,384,128]{2,1,0:T(8,128)(2,1)S(1)}, u32[]{:S(2)}, u32[]{:S(2)}) async-start(bf16[8,384,128]{2,1,0:T(8,128)(2,1)} %bitcast.66), calls=%async_computation.10 | async-start | bytes 1572864 | tf_op jit(solution)/shard_map/all_to_all | solution.py:17
  235.3 2.1 copy.68
  238.6 2.3 fusion.63
  241.6 14.2 %all-to-all-done.10 = bf16[8,384,128]{2,1,0:T(8,128)(2,1)S(1)} async-done(((bf16[8,384,128]{2,1,0:T(8,128)(2,1)}), bf16[8,384,128]{2,1,0:T(8,128)(2,1)S(1)}, u32[]{:S(2)}, u32[]{:S(2)}) %all-to-all-start.10) | async-done | bytes 786464 | tf_op jit(solution)/shard_map/all_to_all | solution.py:17
  255.9 4.0 %collective-permute-start.1 = (bf16[384,128]{1,0:T(8,128)(2,1)S(1)}, bf16[384,128]{1,0:T(8,128)(2,1)S(1)}, u32[]{:S(2)}, u32[]{:S(2)}) collective-permute-start(bf16[384,128]{1,0:T(8,128)(2,1)S(1)} %multiply_convert_fusion.3), channel_id=1, source_target_pairs={{1,32},{3,34},{5,36},{7,38},{9,40},{11,42},{13,44},{15,46},{17,48}... | collective-permute-start | bytes 294920 | tf_op jit(solution)/shard_map/ppermute | solution.py:174
  259.9 2.3 add_convert_fusion.3
  262.2 4.5 %collective-permute-done.1 = bf16[384,128]{1,0:T(8,128)(2,1)S(1)} collective-permute-done((bf16[384,128]{1,0:T(8,128)(2,1)S(1)}, bf16[384,128]{1,0:T(8,128)(2,1)S(1)}, u32[]{:S(2)}, u32[]{:S(2)}) %collective-permute-start.1) | collective-permute-done | bytes 98336 | tf_op jit(solution)/shard_map/ppermute | solution.py:174
  (153 shorter events, 31.1 us)
Async XLA Ops:
  0.6 1.9 copy-start
  2.5 5.9 %copy-start.6 = (bf16[1,8,8,16,128]{4,3,2,1,0:T(8,128)(2,1)S(1)}, bf16[1,8,8,16,128]{4,3,2,1,0:T(8,128)(2,1)}, u32[]{:S(2)}) copy-start(bf16[1,8,8,16,128]{4,3,2,1,0:T(8,128)(2,1)} %param.4) | copy-start | bytes 786436
  8.0 20.8 %collective-permute-start = (bf16[3072,128]{1,0:T(8,128)(2,1)}, bf16[3072,128]{1,0:T(8,128)(2,1)}, u32[]{:S(2)}, u32[]{:S(2)}) collective-permute-start(bf16[3072,128]{1,0:T(8,128)(2,1)} %pad_maximum_fusion.2), channel_id=1, source_target_pairs={{0,129},{1,128},{2,131},{3,130},{4,133},{5,132},{6,135},{7,134},{8... | collective-permute-start | bytes 2359304 | tf_op jit(solution)/shard_map/ppermute | solution.py:106
  30.1 6.0 %copy-start.13 = (bf16[1,8,8,16,128]{4,3,2,1,0:T(8,128)(2,1)S(1)}, bf16[1,8,8,16,128]{4,3,2,1,0:T(8,128)(2,1)}, u32[]{:S(2)}) copy-start(bf16[1,8,8,16,128]{4,3,2,1,0:T(8,128)(2,1)} %param.5) | copy-start | bytes 786436
  37.2 19.1 %all-to-all-start.3 = ((bf16[4,1024,128]{2,1,0:T(8,128)(2,1)}), bf16[4,1024,128]{2,1,0:T(8,128)(2,1)}, u32[]{:S(2)}, u32[]{:S(2)}) async-start(bf16[4,1024,128]{2,1,0:T(8,128)(2,1)} %broadcast_in_dim.32), calls=%async_computation.3 | async-start | bytes 2097152 | tf_op jit(solution)/shard_map/all_to_all | solution.py:17
  43.4 1.3 slice-start
  44.7 1.0 slice-start.1
  44.9 34.3 %copy-start.2 = (bf16[9,2,2,128,128]{4,3,2,1,0:T(8,128)(2,1)}, bf16[9,2,2,128,128]{4,3,2,1,0:T(8,128)(2,1)S(1)}, u32[]{:S(2)}) copy-start(bf16[9,2,2,128,128]{4,3,2,1,0:T(8,128)(2,1)S(1)} %copy.63) | copy-start | bytes 3538948
  57.4 18.8 %all-to-all-start = ((bf16[4,1024,128]{2,1,0:T(8,128)(2,1)}), bf16[4,1024,128]{2,1,0:T(8,128)(2,1)}, u32[]{:S(2)}, u32[]{:S(2)}) async-start(bf16[4,1024,128]{2,1,0:T(8,128)(2,1)} %broadcast_in_dim.28), calls=%async_computation | async-start | bytes 2097152 | tf_op jit(solution)/shard_map/all_to_all | solution.py:17
  63.0 1.5 copy-start.11
  63.0 1.5 copy-start.12
  64.3 0.8 copy-start.14
  64.3 0.8 copy-start.16
  64.3 0.9 copy-start.18
  64.3 0.9 copy-start.20
  64.5 1.2 copy-start.4
  82.0 7.8 %copy-start.5 = (bf16[1024,512]{1,0:T(8,128)(2,1)S(1)}, bf16[1024,512]{1,0:T(8,128)(2,1)}, u32[]{:S(2)}) copy-start(bf16[1024,512]{1,0:T(8,128)(2,1)} %copy-done.4) | copy-start | bytes 3145732
  85.0 9.4 %all-to-all-start.2 = ((bf16[2,1024,128]{2,1,0:T(8,128)(2,1)}), bf16[2,1024,128]{2,1,0:T(8,128)(2,1)S(1)}, u32[]{:S(2)}, u32[]{:S(2)}) async-start(bf16[2,1024,128]{2,1,0:T(8,128)(2,1)} %copy.65), calls=%async_computation.2 | async-start | bytes 1048576 | tf_op jit(solution)/shard_map/all_to_all | solution.py:17
  94.3 11.6 %all-to-all-start.4 = ((bf16[2,1024,128]{2,1,0:T(8,128)(2,1)}), bf16[2,1024,128]{2,1,0:T(8,128)(2,1)S(1)}, u32[]{:S(2)}, u32[]{:S(2)}) async-start(bf16[2,1024,128]{2,1,0:T(8,128)(2,1)} %bitcast.30), calls=%async_computation.4 | async-start | bytes 1048576 | tf_op jit(solution)/shard_map/all_to_all | solution.py:17
  109.2 9.0 %copy-start.3 = (bf16[9,2,2,128,128]{4,3,2,1,0:T(8,128)(2,1)S(1)}, bf16[9,2,2,128,128]{4,3,2,1,0:T(8,128)(2,1)}, u32[]{:S(2)}) copy-start(bf16[9,2,2,128,128]{4,3,2,1,0:T(8,128)(2,1)} %copy-done.2) | copy-start | bytes 3538948
  110.2 16.0 %all-to-all-start.5 = ((bf16[2,2048,128]{2,1,0:T(8,128)(2,1)}), bf16[2,2048,128]{2,1,0:T(8,128)(2,1)}, u32[]{:S(2)}, u32[]{:S(2)}) async-start(bf16[2,2048,128]{2,1,0:T(8,128)(2,1)} %broadcast_in_dim.72), calls=%async_computation.5 | async-start | bytes 2097152 | tf_op jit(solution)/shard_map/all_to_all | solution.py:17
  132.5 2.3 copy-start.15
  132.5 2.3 copy-start.17
  132.5 2.3 copy-start.19
  132.6 2.3 copy-start.21
  135.9 2.4 copy-start.22
  135.9 2.3 copy-start.23
  135.9 2.3 copy-start.24
  135.9 2.3 copy-start.25
  136.1 2.1 copy-start.26
  156.5 9.0 %all-to-all-start.8 = ((bf16[2,6144,128]{2,1,0:T(8,128)(2,1)}), bf16[2,6144,128]{2,1,0:T(8,128)(2,1)}, u32[]{:S(2)}, u32[]{:S(2)}) async-start(bf16[2,6144,128]{2,1,0:T(8,128)(2,1)} %bitcast.133), calls=%async_computation.8 | async-start | bytes 6291456 | tf_op jit(solution)/shard_map/all_to_all | solution.py:17
  165.4 19.5 %all-to-all-start.6 = ((bf16[4,1024,128]{1,2,0:T(8,128)(2,1)}), bf16[4,1024,128]{1,2,0:T(8,128)(2,1)S(1)}, u32[]{:S(2)}, u32[]{:S(2)}) async-start(bf16[4,1024,128]{1,2,0:T(8,128)(2,1)} %bitcast.37), calls=%async_computation.6 | async-start | bytes 2097152 | tf_op jit(solution)/shard_map/all_to_all | solution.py:17
  173.9 15.9 %copy-start.8 = (bf16[9,512,128]{2,1,0:T(8,128)(2,1)S(1)}, bf16[9,512,128]{2,1,0:T(8,128)(2,1)}, u32[]{:S(2)}) copy-start(bf16[9,512,128]{2,1,0:T(8,128)(2,1)} %get-tuple-element.9) | copy-start | bytes 3538948
  184.9 4.9 %copy-start.9 = (bf16[4,1024,128]{1,2,0:T(8,128)(2,1)}, bf16[4,1024,128]{1,2,0:T(8,128)(2,1)S(1)}, u32[]{:S(2)}) copy-start(bf16[4,1024,128]{1,2,0:T(8,128)(2,1)S(1)} %all-to-all-done.6) | copy-start | bytes 3145732
  184.9 22.7 %all-to-all-start.9 = ((bf16[2,3072,128]{2,1,0:T(8,128)(2,1)}), bf16[2,3072,128]{2,1,0:T(8,128)(2,1)}, u32[]{:S(2)}, u32[]{:S(2)}) async-start(bf16[2,3072,128]{2,1,0:T(8,128)(2,1)} %bitcast.65), calls=%async_computation.9 | async-start | bytes 3145728 | tf_op jit(solution)/shard_map/all_to_all | solution.py:17
  207.6 18.1 %all-to-all-start.7 = ((bf16[4,1024,128]{1,2,0:T(8,128)(2,1)}), bf16[4,1024,128]{1,2,0:T(8,128)(2,1)S(1)}, u32[]{:S(2)}, u32[]{:S(2)}) async-start(bf16[4,1024,128]{1,2,0:T(8,128)(2,1)} %bitcast.57), calls=%async_computation.7 | async-start | bytes 2097152 | tf_op jit(solution)/shard_map/all_to_all | solution.py:17
  212.6 21.7 %copy-start.10 = (bf16[4,1024,128]{1,2,0:T(8,128)(2,1)S(1)}, bf16[4,1024,128]{1,2,0:T(8,128)(2,1)}, u32[]{:S(2)}) copy-start(bf16[4,1024,128]{1,2,0:T(8,128)(2,1)} %copy-done.9) | copy-start | bytes 3145732
  225.8 30.0 %all-to-all-start.10 = ((bf16[8,384,128]{2,1,0:T(8,128)(2,1)}), bf16[8,384,128]{2,1,0:T(8,128)(2,1)S(1)}, u32[]{:S(2)}, u32[]{:S(2)}) async-start(bf16[8,384,128]{2,1,0:T(8,128)(2,1)} %bitcast.66), calls=%async_computation.10 | async-start | bytes 1572864 | tf_op jit(solution)/shard_map/all_to_all | solution.py:17
  235.3 3.3 %copy-start.7 = (bf16[1,8,8,16,128]{4,3,2,1,0:T(8,128)(2,1)S(1)}, bf16[1,8,8,16,128]{4,3,2,1,0:T(8,128)(2,1)}, u32[]{:S(2)}) copy-start(bf16[1,8,8,16,128]{4,3,2,1,0:T(8,128)(2,1)} %param.4) | copy-start | bytes 786436
  238.6 29.5 %copy-start.1 = (bf16[3,3,1024,128]{3,2,1,0:T(8,128)(2,1)S(1)}, bf16[3,3,1024,128]{3,2,1,0:T(8,128)(2,1)}, u32[]{:S(2)}) copy-start(bf16[3,3,1024,128]{3,2,1,0:T(8,128)(2,1)} %param.6) | copy-start | bytes 7077892
  255.9 10.8 %collective-permute-start.1 = (bf16[384,128]{1,0:T(8,128)(2,1)S(1)}, bf16[384,128]{1,0:T(8,128)(2,1)S(1)}, u32[]{:S(2)}, u32[]{:S(2)}) collective-permute-start(bf16[384,128]{1,0:T(8,128)(2,1)S(1)} %multiply_convert_fusion.3), channel_id=1, source_target_pairs={{1,32},{3,34},{5,36},{7,38},{9,40},{11,42},{13,44},{15,46},{17,48}... | collective-permute-start | bytes 294920 | tf_op jit(solution)/shard_map/ppermute | solution.py:174

commit v2 on v0

v2 whole, which is shorter than its diff:
```python
import jax
import jax.numpy as jnp
from jax import lax
from jax.experimental import pallas as pl
from jax.experimental.pallas import tpu as pltpu
from jax.sharding import PartitionSpec as P

GS = 32
ROWS = 1024
BF = jnp.bfloat16
F32 = jnp.float32
NT = (((1,), (1,)), ((), ()))
Z_GROUPS = [[l * 16 + z * 2 + c for z in range(8)] for l in range(2) for c in range(2)]


def tensor_move(values, y_step, x_flip):
    pairs = [(t, ((t // 2 + y_step) % 4) * 2 + (t % 2 ^ x_flip)) for t in range(8)]
    return lax.ppermute(values, "tensor", pairs)


def data_move(values, bits):
    return lax.ppermute(values, "dp", [(d, d ^ bits) for d in range(32)])


def block(index):
    return pl.ds(pl.multiple_of(index * 128, 128), 128)


def call(body, outs, scratch, args, flops, name, unread=0):
    total = sum(a.size * a.dtype.itemsize for a in args)
    total += sum(o.size * o.dtype.itemsize for o in outs)
    smem = pl.BlockSpec(memory_space=pltpu.SMEM)
    vmem = pl.BlockSpec(memory_space=pltpu.VMEM)
    specs = [smem if a.dtype == jnp.int32 else vmem for a in args]
    if unread:
        specs[-unread:] = [pl.BlockSpec(memory_space=pl.ANY)] * unread
    result = pl.pallas_call(
        body,
        out_shape=outs,
        in_specs=specs,
        out_specs=[vmem] * len(outs),
        scratch_shapes=scratch,
        compiler_params=pltpu.CompilerParams(vmem_limit_bytes=48 * 1024 * 1024),
        cost_estimate=pl.CostEstimate(flops=flops, bytes_accessed=total, transcendentals=0),
        name=name,
    )(*args)
    return list(result)


def shape(dims, dtype):
    return jax.ShapeDtypeStruct(dims, dtype)


def group_mean(values):
    sums = jnp.sum(values, axis=0, keepdims=True)
    rows = lax.broadcasted_iota(jnp.int32, (128, 128), 0) // GS
    lanes = lax.broadcasted_iota(jnp.int32, (128, 128), 1) // GS
    same = (rows == lanes).astype(F32)
    sums = jnp.broadcast_to(sums, (8, 128))
    sums = jnp.dot(sums, same, precision=lax.Precision.HIGHEST, preferred_element_type=F32)
    return sums[0:1] * (1.0 / (ROWS * GS))


def normalize(values):
    offsets = values - group_mean(values)
    scale = lax.rsqrt(group_mean(offsets * offsets) + 1e-05)
    return offsets * scale, scale


def gate_of(unit):
    return 1.0 / (1.0 + jnp.exp(-unit))


def act_back(unit, scale, gate, grads):
    inner = grads * (gate * (1.0 + unit * (1.0 - gate)))
    return scale * (inner - group_mean(inner) - unit * group_mean(inner * unit))


def first_act_kernel(clips, after, hidden):
    unit, _ = normalize(clips[...].astype(F32))
    hidden[...] = (unit * gate_of(unit)).astype(BF)


def second_act_kernel(out_own, out_got, grad_own, grad_got, both):
    unit, scale = normalize(out_own[...] + out_got[...].astype(F32))
    gate = gate_of(unit)
    both[1] = (unit * gate).astype(BF)
    received = grad_own[...] + grad_got[...].astype(F32)
    both[0] = act_back(unit, scale, gate, received).astype(BF)


def finish_kernel(clips, out_grad, own_back, own_ahead, got_a, got_b, got_c, mixed, clip_grad):
    rows = clips[...].astype(F32)
    ahead = own_ahead[...] + got_a[1].astype(F32) + got_b[1].astype(F32) + got_c[1].astype(F32)
    mixed[...] = (rows + ahead).astype(BF)
    unit, scale = normalize(rows)
    grads = own_back[...] + got_a[0].astype(F32) + got_b[0].astype(F32) + got_c[0].astype(F32)
    back = act_back(unit, scale, gate_of(unit), grads)
    clip_grad[...] = (out_grad[...].astype(F32) + back).astype(BF)


def unfold(values, target, column, steps=(-1, 0, 1)):
    wide = values.astype(F32)
    place = lax.broadcasted_iota(jnp.int32, (ROWS, 128), 0) % 16
    for sb in (-1, 0, 1):
        moved = wide
        if sb:
            moved = pltpu.roll(wide, (-sb) % ROWS, 0)
            moved = jnp.where(place == (15 if sb == 1 else 0), 0.0, moved)
        moved = moved.astype(BF).reshape(8, 128, 128)
        zeros = jnp.zeros((8, 16, 128), BF)
        for sa in steps:
            at = column(sa, sb)
            if sa == 0:
                target[:, :, at] = moved
            elif sa == 1:
                target[:, 0:112, at] = moved[:, 16:]
                target[:, 112:128, at] = zeros
            else:
                target[:, 16:128, at] = moved[:, :112]
                target[:, 0:16, at] = zeros


def frames(values, target, column):
    zeros = jnp.zeros((128, 128), BF)
    for s in (-1, 0, 1):
        at = column(s)
        if s == 0:
            target[:, at] = values
        elif s == 1:
            target[0:896, at] = values[128:]
            target[896:1024, at] = zeros
        else:
            target[128:1024, at] = values[:896]
            target[0:128, at] = zeros


def temporal_pair(place, weight, got_a, got_b, pair):
    x_hi, core = place[1], place[2]
    for k in range(3):
        for yb in range(4):
            pair[k, 0:128, yb * 128 : yb * 128 + 128] = weight[k, :, block(2 * yb + x_hi)]
        for j in range(2):
            pair[k, 128:256, block(2 * core + j)] = got_a[k, j]
            pair[k, 128:256, block(2 - 2 * core + j)] = got_b[k, j]


def spatial_give_kernel(place, weight, give):
    x_hi, core = place[1], place[2]
    for j in range(2):
        at = block(2 * (2 * core + j) + 1 - x_hi)
        for tap in range(9):
            give[tap, j] = weight[tap, at, :]


def temporal_give_kernel(place, weight, after, give):
    x_hi, core = place[1], place[2]
    for j in range(2):
        at = block(2 * (2 * core + j) + 1 - x_hi)
        for k in range(3):
            give[k, j] = weight[k, :, at]


def spatial_pair_kernel(place, weight, got_a, got_b, pair):
    x_hi, core = place[1], place[2]
    for tap in range(9):
        for yb in range(4):
            at = tap * 512 + yb * 128
            pair[at : at + 128, 0:128] = weight[tap, block(2 * yb + x_hi), :]
        for j in range(2):
            pair[block(tap * 4 + 2 * core + j), 128:256] = got_a[tap, j]
            pair[block(tap * 4 + 2 - 2 * core + j), 128:256] = got_b[tap, j]


def grad_second_kernel(
    place, g0, g1, g2, g3, weight, got_a, got_b, after, own, give, pair, wide
):
    y = place[0]
    temporal_pair(place, weight, got_a, got_b, pair)
    for d, piece in enumerate((g0, g1, g2, g3)):
        yb = lax.rem(y - d + 4, 4)
        frames(piece[...], wide, lambda s: block((1 - s) * 4 + yb))

    def step(i, carry):
        rows = pl.ds(pl.multiple_of(i * 256, 256), 256)
        total = jnp.zeros((256, 256), F32)
        for k in range(3):
            total += lax.dot_general(
                wide[rows, k * 512 : k * 512 + 512], pair[k], NT, preferred_element_type=F32
            )
        own[rows, :] = total[:, :128]
        give[rows, :] = total[:, 128:].astype(BF)
        return carry

    lax.fori_loop(0, 4, step, 0)


def spatial_out_kernel(place, h0, h1, h2, h3, pair, own, give, wide):
    y = place[0]
    for d, piece in enumerate((h0, h1, h2, h3)):
        yb = lax.rem(y - d + 4, 4)
        unfold(piece[...], wide, lambda sa, sb: block(((sa + 1) * 3 + sb + 1) * 4 + yb))

    def step(i, carry):
        rows = pl.ds(pl.multiple_of(i * 256, 256), 256)
        left = wide[pl.ds(2 * i, 2)].reshape(256, 4608)
        total = jnp.dot(left, pair[...], preferred_element_type=F32)
        own[rows, :] = total[:, :128]
        give[rows, :] = total[:, 128:].astype(BF)
        return carry

    lax.fori_loop(0, 4, step, 0)


def both_back_kernel(
    place, b0, b1, spatial, temporal, got_a, got_b, after,
    own_back, own_ahead, o1, o2, o3, pair, wide, pair_t, wide_t, total
):
    y = place[0]
    for tap in range(9):
        pair[:, tap * 256 : tap * 256 + 256] = spatial[tap * 512 : tap * 512 + 512, :]
    fill_grads((b0, b1), wide, (1, 0, -1))
    temporal_pair(place, temporal, got_a, got_b, pair_t)
    for j, piece in enumerate((b0, b1)):
        frames(piece[1], wide_t, lambda s: slice((s + 1) * 256 + j * 128, (s + 1) * 256 + j * 128 + 128))

    def spread(rows, own, part):
        own[rows, :] = total[:, block(y)]
        for d, out in enumerate((o1, o2, o3)):
            out[part, rows, :] = total[:, block(lax.rem(y + d + 1, 4))].astype(BF)

    def step(i, carry):
        rows = pl.ds(pl.multiple_of(i * 256, 256), 256)
        left = wide[pl.ds(2 * i, 2)].reshape(256, 2304)
        total[...] = lax.dot_general(left, pair[...], NT, preferred_element_type=F32)
        spread(rows, own_back, 0)
        total[...] = jnp.dot(
            wide_t[rows, :], pair_t[...].reshape(768, 512), preferred_element_type=F32
        )
        spread(rows, own_ahead, 1)
        return carry

    lax.fori_loop(0, 4, step, 0)


def fill_grads(pieces, wide, steps):
    for j, piece in enumerate(pieces):

        def column(sa, sb):
            at = (steps.index(sa) * 3 + 1 - sb) * 256 + j * 128
            return slice(at, at + 128)

        unfold(piece[0], wide, column, steps)


def transposed(y, pieces, target):
    for d, piece in enumerate(pieces):
        target[block(lax.rem(y - d + 4, 4)), :] = piece[...].T


def place_tap(place, total, keep, give, tap):
    x_hi, core, x_lo = place[1], place[2], place[3]
    for xr in range(2):
        for z in range(8):
            z2, z1, z0 = z // 4, z // 2 % 2, z % 2
            row = (lax.rem(x_lo + xr, 2) * 2 + z2) * 128 + z0 * 64
            col = block(lax.rem(x_hi + z1, 2))
            mine = pl.ds(pl.multiple_of(row + core * 32, 32), 32)
            other = pl.ds(pl.multiple_of(row + 32 - core * 32, 32), 32)
            keep[xr, z, tap] = total[mine, col]
            give[xr, z, tap] = total[other, col].astype(BF)


def spatial_taps(place, first, wide, keep, give, total, taps):
    def step(tap, carry):
        cols = pl.ds(pl.multiple_of(tap * 256, 256), 256)
        total[...] = jnp.dot(
            first[...], wide[:, :, cols].reshape(ROWS, 256), preferred_element_type=F32
        )
        place_tap(place, total, keep, give, tap)
        return carry

    lax.fori_loop(0, taps, step, 0)


def early_grads_kernel(place, h0, h1, h2, h3, b0, b1, keep, give, first, wide, total):
    transposed(place[0], (h0, h1, h2, h3), first)
    fill_grads((b0, b1), wide, (1, 0))
    spatial_taps(place, first, wide, keep, give, total, 6)


def late_grads_kernel(
    place, h0, h1, h2, h3, g0, g1, g2, g3, b0, b1, after, keep, give, first, grads, wide, tall, total
):
    transposed(place[0], (h0, h1, h2, h3), first)
    transposed(place[0], (g0, g1, g2, g3), grads)
    fill_grads((b0, b1), wide, (-1,))
    for j, piece in enumerate((b0, b1)):
        frames(piece[1], tall, lambda s: slice((s + 1) * 256 + j * 128, (s + 1) * 256 + j * 128 + 128))
    spatial_taps(place, first, wide, keep, give, total, 3)

    def step(tap, carry):
        cols = pl.ds(pl.multiple_of(tap * 256, 256), 256)
        total[...] = jnp.dot(grads[...], tall[:, cols], preferred_element_type=F32)
        place_tap(place, total, keep, give, tap + 3)
        return carry

    lax.fori_loop(0, 3, step, 0)


def core_sum(keep, give):
    got = data_move(give, 1).astype(F32)
    return keep[0] + got[0], (keep[1] + got[1]).astype(BF)


def x_lo_sum(keep, give):
    return (keep + data_move(give, 16).astype(F32)).astype(BF)


def per_device(clips, out_grad, spatial_weight, temporal_weight):
    tensor, data = lax.axis_index("tensor"), lax.axis_index("dp")
    x_hi, core = tensor % 2, data % 2
    z_mid = (data // 4) % 2
    place = jnp.stack([tensor // 2, x_hi, core, data // 16]).astype(jnp.int32)
    grad_scale = 1.0 / jnp.sqrt(jnp.float32(32768))
    clip_rows = clips.reshape(ROWS, 128)
    grads = out_grad.reshape(ROWS, 128)
    spatial = spatial_weight.reshape(9, 1024, 128)
    temporal = temporal_weight
    piece, wide_piece = shape((ROWS, 128), BF), shape((ROWS, 128), F32)

    cross = [
        (d * 8 + t, ((d + 16) % 32) * 8 + (t ^ 1)) for d in range(32) for t in range(8)
    ]
    (spatial_give,) = call(
        spatial_give_kernel, [shape((9, 2, 128, 128), BF)], [], [place, spatial], 0, "spatial_give"
    )
    (hidden_first,) = call(
        first_act_kernel, [piece], [], [clip_rows, spatial_give], 10**6, "first_act", unread=1
    )
    spatial_a = lax.ppermute(spatial_give, ("dp", "tensor"), cross)
    first_all = [hidden_first] + [tensor_move(hidden_first, d, 0) for d in (1, 2, 3)]
    (temporal_give,) = call(
        temporal_give_kernel,
        [shape((3, 2, 128, 128), BF)],
        [],
        [place, temporal, hidden_first],
        10**6,
        "temporal_give",
        unread=1,
    )
    spatial_a, temporal_give, grads, first_all = lax.optimization_barrier(
        (spatial_a, temporal_give, grads, first_all)
    )
    spatial_b = data_move(spatial_a, 1)
    grads_all = [grads] + [tensor_move(grads, d, 0) for d in (1, 2, 3)]
    temporal_a = lax.ppermute(temporal_give, ("dp", "tensor"), cross)
    temporal_b = data_move(temporal_a, 1)
    temporal_args = [temporal, temporal_a, temporal_b]
    (spatial_pair,) = call(
        spatial_pair_kernel,
        [shape((4608, 256), BF)],
        [],
        [place, spatial, spatial_a, spatial_b],
        10**6,
        "spatial_pair",
    )
    out_own, out_give = call(
        spatial_out_kernel,
        [wide_piece, piece],
        [pltpu.VMEM((8, 128, 4608), BF)],
        [place] + first_all + [spatial_pair],
        2 * ROWS * 4608 * 256,
        "spatial_out",
    )
    out_got = tensor_move(out_give, 0, 1)
    second_own, second_give = call(
        grad_second_kernel,
        [wide_piece, piece],
        [pltpu.VMEM((3, 256, 512), BF), pltpu.VMEM((ROWS, 1536), BF)],
        [place] + grads_all + temporal_args + [out_give],
        2 * ROWS * 1536 * 256,
        "grad_second",
        unread=1,
    )
    second_got = tensor_move(second_give, 0, 1)
    (both,) = call(
        second_act_kernel,
        [shape((2, ROWS, 128), BF)],
        [],
        [out_own, out_got, second_own, second_got],
        10**7,
        "second_act",
    )
    both_pair = [both, tensor_move(both, 0, 1)]

    half = [shape((2, 8, 6, 32, 128), F32), shape((2, 8, 6, 32, 128), BF)]
    keep, give = call(
        early_grads_kernel,
        half,
        [
            pltpu.VMEM((512, ROWS), BF),
            pltpu.VMEM((8, 128, 1536), BF),
            pltpu.VMEM((512, 256), F32),
        ],
        [place] + first_all + both_pair,
        2 * ROWS * 1536 * 512,
        "early_grads",
    )
    late_keep, late_give = call(
        late_grads_kernel,
        half,
        [
            pltpu.VMEM((512, ROWS), BF),
            pltpu.VMEM((512, ROWS), BF),
            pltpu.VMEM((8, 128, 768), BF),
            pltpu.VMEM((ROWS, 768), BF),
            pltpu.VMEM((512, 256), F32),
        ],
        [place] + first_all + grads_all + both_pair + [give],
        2 * ROWS * 1536 * 512,
        "late_grads",
        unread=1,
    )
    early_local = x_lo_sum(*core_sum(keep, give))
    own_back, own_ahead, *parts = call(
        both_back_kernel,
        [wide_piece, wide_piece] + [shape((2, ROWS, 128), BF)] * 3,
        [
            pltpu.VMEM((512, 2304), BF),
            pltpu.VMEM((8, 128, 2304), BF),
            pltpu.VMEM((3, 256, 512), BF),
            pltpu.VMEM((ROWS, 768), BF),
            pltpu.VMEM((256, 512), F32),
        ],
        [place] + both_pair + [spatial_pair] + temporal_args + [late_give],
        2 * ROWS * 3072 * 512,
        "both_back",
        unread=1,
    )

    late_local = x_lo_sum(*core_sum(late_keep, late_give))
    local = jnp.concatenate([early_local, late_local], axis=1)
    local, parts = lax.optimization_barrier((local, parts))
    parts = [tensor_move(parts[d - 1], d, 0) for d in (1, 2, 3)]
    local = lax.all_to_all(
        local,
        "dp",
        split_axis=0,
        concat_axis=0,
        tiled=True,
        axis_index_groups=Z_GROUPS,
    )
    share = (jnp.sum(local.astype(F32), axis=0) * grad_scale).astype(BF)
    move = []
    for d in range(32):
        for t in range(8):
            if (d // 4) % 2 != t % 2:
                move.append((d * 8 + t, (d ^ 4) * 8 + (t ^ 1)))
    moved = lax.ppermute(share, ("dp", "tensor"), move)
    share = jnp.where(z_mid == x_hi, share, moved)
    spatial_share = share[:9].reshape(3, 3, 32, 128)
    temporal_share = share[9:].swapaxes(1, 2)

    mixed, clip_grad = call(
        finish_kernel,
        [piece, piece],
        [],
        [clip_rows, grads, own_back, own_ahead] + parts,
        10**7,
        "finish",
    )
    return (
        mixed.reshape(clips.shape),
        clip_grad.reshape(clips.shape),
        spatial_share,
        temporal_share,
    )


def solution(mesh):
    placed = (
        P("dp", None, None, None, "tensor"),
        P("dp", None, None, None, "tensor"),
        P(None, None, None, "tensor"),
        P(None, "tensor", None),
    )
    return jax.shard_map(
        per_device,
        mesh=mesh,
        in_specs=placed,
        out_specs=(
            P("dp", None, None, None, "tensor"),
            P("dp", None, None, None, "tensor"),
            P(None, None, "dp", "tensor"),
            P(None, "tensor", "dp"),
        ),
        check_vma=False,
    )
```

time: 702 us -> 150 us (0.21)
  waiting for transfers between devices: 610 us -> 75.1 us
  matrix products: 35.4 us -> 0 us
  Pallas kernels: 0 us -> 34 us
  starting transfers between devices: 0.47 us -> 33.3 us
  local copies, waits for them, and re-layouts: 24 us -> 2.94 us
  between operations: 15 us -> 0.96 us
  other arithmetic: 15.9 us -> 3.52 us
    reduce_scatter x3 -> x0, waiting for transfers between devices: 303 us -> none  [the longest x1 123 us: per_device(): lax.psum_scatter(spatial_local, 'dp', scatter_dimension=2, tiled=True)]
    unnamed x7 -> x0, waiting for transfers between devices: 197 us -> none
    all_gather x2 -> x0, waiting for transfers between devices: 110 us -> none  [the longest x1 57.7 us: per_device(): first_full = lax.all_gather(hidden_first, 'tensor', axis=4, tiled=True)]
    ppermute x0 -> x21, waiting for transfers between devices: none -> 57.4 us  [the longest x12 39.8 us: tensor_move(): return lax.ppermute(values, 'tensor', pairs)]
    pallas_call x0 -> x11, Pallas kernels: none -> 34 us  [call(): pl.pallas_call(body, out_shape=outs, in_specs=specs, out_specs=[vmem] * l...]
    ppermute x0 -> x21, starting transfers between devices: none -> 24.8 us  [the longest x12 18.3 us: tensor_move(): return lax.ppermute(values, 'tensor', pairs)]
    dot_general x18 -> x0, matrix products: 24.3 us -> none  [the longest x9 17 us: spatial_wgrad(): lax.dot_general(window, right_side, (((0,), (0,)), ((), ())), preferred_e...]
    all_to_all x0 -> x1, waiting for transfers between devices: none -> 17.7 us  [per_device(): lax.all_to_all(local, 'dp', split_axis=0, concat_axis=0, tiled=True, axis...]
  transfers between devices with their start and end apart: 6 -> 22, of which waited for: 6 -> 13; matrix products, arithmetic and copies ran while one was open for 7% -> 1% of each run, Pallas kernels for 0% -> 16%
where the time goes in v2:
time: 150 us
  waiting for transfers between devices  75.1 us (50%)
  Pallas kernels  34 us (23%)
  starting transfers between devices  33.3 us (22%)
  other arithmetic  3.52 us (2%)
  local copies, waits for them, and re-layouts  2.94 us (2%)
    ppermute x12, waiting for transfers between devices, tensor_move(): return lax.ppermute(values, 'tensor', pairs)  39.8 us
    pallas_call x11, Pallas kernels, call(): pl.pallas_call(body, out_shape=outs, in_specs=specs, out_specs=[vmem] * l...  34 us
    ppermute x12, starting transfers between devices, tensor_move(): return lax.ppermute(values, 'tensor', pairs)  18.3 us
    all_to_all x1, waiting for transfers between devices, per_device(): lax.all_to_all(local, 'dp', split_axis=0, concat_axis=0, tiled=True, axis...  17.7 us
    ppermute x6, waiting for transfers between devices, data_move(): return lax.ppermute(values, 'dp', [(d, d ^ bits) for d in range(32)])  9.77 us
    all_to_all x1, starting transfers between devices, per_device(): lax.all_to_all(local, 'dp', split_axis=0, concat_axis=0, tiled=True, axis...  8.47 us
    ppermute x1, waiting for transfers between devices, per_device(): moved = lax.ppermute(share, ('dp', 'tensor'), move)  6.46 us
  transfers between devices with their start and end apart: 22, of which 13 were waited for; matrix products, arithmetic and copies ran while one was open for 1% of the time, Pallas kernels for 16%

profile of v2, /device:TPU:14, one launch (start us, length us, event | category | flops | bytes accessed | tf_op | source)
XLA Modules:
  0.0 149.8 jit_solution(8579220871989505616)
XLA Ops:
  0.7 1.7 %copy-done = bf16[3,3,1024,128]{3,2,1,0:T(8,128)(2,1)S(1)} copy-done((bf16[3,3,1024,128]{3,2,1,0:T(8,128)(2,1)S(1)}, bf16[3,3,1024,128]{3,2,1,0:T(8,128)(2,1)}, u32[]{:S(2)}) %copy-start) | copy-done | bytes 2359320
  2.4 0.6 spatial_give.1.after
  3.0 0.6 collective-permute-start
  3.6 0.8 first_act.1.after.h0
  4.4 1.7 %collective-permute-start.1 = (bf16[1024,128]{1,0:T(8,128)(2,1)S(1)}, bf16[1024,128]{1,0:T(8,128)(2,1)S(1)}, u32[]{:S(2)}, u32[]{:S(2)}) collective-permute-start(bf16[1024,128]{1,0:T(8,128)(2,1)S(1)} %first_act.1.after.h0), channel_id=1, source_target_pairs={{0,2},{1,3},{2,4},{3,5},{4,6},{5,7},{6,0},{7,1},{8,10},{9,11},{10,... | collective-permute-start | bytes 786440 | tf_op jit(solution)/shard_map/ppermute | solution.py:18
  6.1 2.7 %collective-permute-start.2 = (bf16[1024,128]{1,0:T(8,128)(2,1)S(1)}, bf16[1024,128]{1,0:T(8,128)(2,1)S(1)}, u32[]{:S(2)}, u32[]{:S(2)}) collective-permute-start(bf16[1024,128]{1,0:T(8,128)(2,1)S(1)} %first_act.1.after.h0), channel_id=1, source_target_pairs={{0,4},{1,5},{2,6},{3,7},{4,0},{5,1},{6,2},{7,3},{8,12},{9,13},{10,... | collective-permute-start | bytes 786440 | tf_op jit(solution)/shard_map/ppermute | solution.py:18
  8.8 0.7 collective-permute-start.3
  9.5 0.6 temporal_give.1
  10.1 3.9 %collective-permute-done.1.h1 = bf16[1024,128]{1,0:T(8,128)(2,1)S(1)} collective-permute-done((bf16[1024,128]{1,0:T(8,128)(2,1)S(1)}, bf16[1024,128]{1,0:T(8,128)(2,1)S(1)}, u32[]{:S(2)}, u32[]{:S(2)}) %collective-permute-start.1) | collective-permute-done | bytes 262176 | tf_op jit(solution)/shard_map/ppermute | solution.py:18
  13.9 2.9 %collective-permute-done.2.h2 = bf16[1024,128]{1,0:T(8,128)(2,1)S(1)} collective-permute-done((bf16[1024,128]{1,0:T(8,128)(2,1)S(1)}, bf16[1024,128]{1,0:T(8,128)(2,1)S(1)}, u32[]{:S(2)}, u32[]{:S(2)}) %collective-permute-start.2) | collective-permute-done | bytes 262176 | tf_op jit(solution)/shard_map/ppermute | solution.py:18
  16.9 3.2 %collective-permute-done.3.h3 = bf16[1024,128]{1,0:T(8,128)(2,1)S(1)} collective-permute-done((bf16[1024,128]{1,0:T(8,128)(2,1)S(1)}, bf16[1024,128]{1,0:T(8,128)(2,1)S(1)}, u32[]{:S(2)}, u32[]{:S(2)}) %collective-permute-start.3) | collective-permute-done | bytes 262176 | tf_op jit(solution)/shard_map/ppermute | solution.py:18
  20.1 2.7 %collective-permute-start.9 = (bf16[3,2,128,128]{3,2,1,0:T(8,128)(2,1)S(1)}, bf16[3,2,128,128]{3,2,1,0:T(8,128)(2,1)S(1)}, u32[]{:S(2)}, u32[]{:S(2)}) collective-permute-start(bf16[3,2,128,128]{3,2,1,0:T(8,128)(2,1)S(1)} %temporal_give.1), channel_id=1, source_target_pairs={{0,129},{1,128},{2,131},{3,130},{4,133},{5,132},{6,135},{7,134},{8... | collective-permute-start | bytes 589832 | tf_op jit(solution)/shard_map/ppermute | solution.py:357
  22.8 1.3 collective-permute-start.6
  24.1 1.7 %collective-permute-start.7 = (bf16[1024,128]{1,0:T(8,128)(2,1)S(1)}, bf16[1024,128]{1,0:T(8,128)(2,1)S(1)}, u32[]{:S(2)}, u32[]{:S(2)}) collective-permute-start(bf16[1024,128]{1,0:T(8,128)(2,1)S(1)} %bitcast.33), channel_id=1, source_target_pairs={{0,4},{1,5},{2,6},{3,7},{4,0},{5,1},{6,2},{7,3},{8,12},{9,13},{10,... | collective-permute-start | bytes 786440 | tf_op jit(solution)/shard_map/ppermute | solution.py:18
  25.7 1.5 collective-permute-start.8
  27.2 1.4 collective-permute-done.9.got_a
  28.6 1.0 spatial_pair.1.pair.spatial
  29.6 5.4 %spatial_out.1 = (f32[1024,128]{1,0:T(8,128)S(1)}, bf16[1024,128]{1,0:T(8,128)(2,1)S(1)}) custom-call(s32[4]{0:T(128)S(1)} %pad_add_fusion.place, bf16[1024,128]{1,0:T(8,128)(2,1)S(1)} %first_act.1.after.h0, bf16[1024,128]{1,0:T(8,128)(2,1)S(1)} %collective-permute-done.1.h1, bf16[1024,128]{1,0:T(8,128)(2,1)S(1)} %collective-permute-done.2.h2, ...), custom_call_target="tpu_custom_call" | custom-call | flops 2415919104 | bytes 4194320 | tf_op jit(solution)/shard_map/spatial_out/pallas_call | solution.py:37
  35.0 4.2 %collective-permute-done.8.g3 = bf16[1024,128]{1,0:T(8,128)(2,1)S(1)} collective-permute-done((bf16[1024,128]{1,0:T(8,128)(2,1)S(1)}, bf16[1024,128]{1,0:T(8,128)(2,1)S(1)}, u32[]{:S(2)}, u32[]{:S(2)}) %collective-permute-start.8) | collective-permute-done | bytes 262176 | tf_op jit(solution)/shard_map/ppermute | solution.py:18
  39.2 2.8 %grad_second.1 = (f32[1024,128]{1,0:T(8,128)S(1)}, bf16[1024,128]{1,0:T(8,128)(2,1)S(1)}) custom-call(s32[4]{0:T(128)S(1)} %pad_add_fusion.place, bf16[1024,128]{1,0:T(8,128)(2,1)S(1)} %bitcast.35, bf16[1024,128]{1,0:T(8,128)(2,1)S(1)} %collective-permute-done.6.g1, bf16[1024,128]{1,0:T(8,128)(2,1)S(1)} %collective-permute-done.7.g2, ...), custom_call_target="tpu_custom_call" | custom-call | flops 805306368 | bytes 3276816 | tf_op jit(solution)/shard_map/grad_second/pallas_call | solution.py:37
  42.0 0.3 collective-permute-start.11
  42.3 3.3 %collective-permute-start.5 = (bf16[1024,128]{1,0:T(8,128)(2,1)S(1)}, bf16[1024,128]{1,0:T(8,128)(2,1)S(1)}, u32[]{:S(2)}, u32[]{:S(2)}) collective-permute-start(bf16[1024,128]{1,0:T(8,128)(2,1)S(1)} %get-tuple-element.37.after), channel_id=1, source_target_pairs={{0,1},{1,0},{2,3},{3,2},{4,5},{5,4},{6,7},{7,6},{8,9},{9,8},{10,11... | collective-permute-start | bytes 786440 | tf_op jit(solution)/shard_map/ppermute | solution.py:18
  45.6 7.2 %collective-permute-done.11.grad_got = bf16[1024,128]{1,0:T(8,128)(2,1)S(1)} collective-permute-done((bf16[1024,128]{1,0:T(8,128)(2,1)S(1)}, bf16[1024,128]{1,0:T(8,128)(2,1)S(1)}, u32[]{:S(2)}, u32[]{:S(2)}) %collective-permute-start.11) | collective-permute-done | bytes 262176 | tf_op jit(solution)/shard_map/ppermute | solution.py:18
  52.8 4.4 %collective-permute-done.5.out_got = bf16[1024,128]{1,0:T(8,128)(2,1)S(1)} collective-permute-done((bf16[1024,128]{1,0:T(8,128)(2,1)S(1)}, bf16[1024,128]{1,0:T(8,128)(2,1)S(1)}, u32[]{:S(2)}, u32[]{:S(2)}) %collective-permute-start.5) | collective-permute-done | bytes 262176 | tf_op jit(solution)/shard_map/ppermute | solution.py:18
  57.2 1.4 second_act.1.b0
  58.7 0.4 collective-permute-start.12
  59.0 14.0 %collective-permute-done.12.b1 = bf16[2,1024,128]{2,1,0:T(8,128)(2,1)S(1)} collective-permute-done((bf16[2,1024,128]{2,1,0:T(8,128)(2,1)S(1)}, bf16[2,1024,128]{2,1,0:T(8,128)(2,1)S(1)}, u32[]{:S(2)}, u32[]{:S(2)}) %collective-permute-start.12) | collective-permute-done | bytes 524320 | tf_op jit(solution)/shard_map/ppermute | solution.py:18
  73.0 4.5 %early_grads.1 = (f32[2,8,6,32,128]{4,3,2,1,0:T(8,128)S(1)}, bf16[2,8,6,32,128]{4,3,2,1,0:T(8,128)(2,1)S(1)}) custom-call(s32[4]{0:T(128)S(1)} %pad_add_fusion.place, bf16[1024,128]{1,0:T(8,128)(2,1)S(1)} %first_act.1.after.h0, bf16[1024,128]{1,0:T(8,128)(2,1)S(1)} %collective-permute-done.1.h1, bf16[1024,128]{1,0:T(8,128)(2,1)S(1)} %collective-permute-done.2.h2, ...), custom_call_target="tpu_custom_call" | custom-call | flops 1610612736 | bytes 4456464 | tf_op jit(solution)/shard_map/early_grads/pallas_call | solution.py:37
  77.7 5.9 %late_grads.1 = (f32[2,8,6,32,128]{4,3,2,1,0:T(8,128)}, bf16[2,8,6,32,128]{4,3,2,1,0:T(8,128)(2,1)S(1)}) custom-call(s32[4]{0:T(128)S(1)} %pad_add_fusion.place, bf16[1024,128]{1,0:T(8,128)(2,1)S(1)} %first_act.1.after.h0, bf16[1024,128]{1,0:T(8,128)(2,1)S(1)} %collective-permute-done.1.h1, bf16[1024,128]{1,0:T(8,128)(2,1)S(1)} %collective-permute-done.2.h2, ...), custom_call_target="tpu_custom_call" | custom-call | flops 1610612736 | bytes 6291472 | tf_op jit(solution)/shard_map/late_grads/pallas_call | solution.py:37
  83.6 0.5 collective-permute-start.15
  84.1 0.2 convert_element_type.36
  84.6 1.4 collective-permute-done.15
  86.0 0.2 convert_element_type.41
  86.4 0.7 collective-permute-start.16
  87.1 8.4 %both_back.1 = (f32[1024,128]{1,0:T(8,128)S(1)}, f32[1024,128]{1,0:T(8,128)S(1)}, bf16[2,1024,128]{2,1,0:T(8,128)(2,1)}, bf16[2,1024,128]{2,1,0:T(8,128)(2,1)}, bf16[2,1024,128]{2,1,0:T(8,128)(2,1)S(1)}) custom-call(s32[4]{0:T(128)S(1)} %pad_add_fusion.place, bf16[2,1024,128]{2,1,0:T(8,128)(2,1)S(1)} %second_act.1.b0, ...), custom_call_target="tpu_custom_call" | custom-call | flops 3221225472 | bytes 7995408 | tf_op jit(solution)/shard_map/both_back/pallas_call | solution.py:37
  95.5 1.1 collective-permute-done.14
  96.7 7.3 %collective-permute-done.16 = bf16[8,6,32,128]{3,2,1,0:T(8,128)(2,1)S(1)} collective-permute-done((bf16[8,6,32,128]{3,2,1,0:T(8,128)(2,1)S(1)}, bf16[8,6,32,128]{3,2,1,0:T(8,128)(2,1)S(1)}, u32[]{:S(2)}, u32[]{:S(2)}) %collective-permute-start.16) | collective-permute-done | bytes 393248 | tf_op jit(solution)/shard_map/ppermute | solution.py:22
  104.2 1.0 pad_maximum_fusion
  105.2 8.5 %all-to-all-start = ((bf16[8,12,32,128]{3,2,1,0:T(8,128)(2,1)}), bf16[8,12,32,128]{3,2,1,0:T(8,128)(2,1)}, u32[]{:S(2)}, u32[]{:S(2)}) async-start(bf16[8,12,32,128]{3,2,1,0:T(8,128)(2,1)} %pad_maximum_fusion), calls=%async_computation | async-start | bytes 1572864 | tf_op jit(solution)/shard_map/all_to_all | solution.py:446
  113.7 2.3 %collective-permute-start.18 = (bf16[2,1024,128]{2,1,0:T(8,128)(2,1)}, bf16[2,1024,128]{2,1,0:T(8,128)(2,1)S(1)}, u32[]{:S(2)}, u32[]{:S(2)}) collective-permute-start(bf16[2,1024,128]{2,1,0:T(8,128)(2,1)} %get-tuple-element.51), channel_id=1, source_target_pairs={{0,4},{1,5},{2,6},{3,7},{4,0},{5,1},{6,2},{7,3},{8,12},{9,13},{10,... | collective-permute-start | bytes 1572872 | tf_op jit(solution)/shard_map/ppermute | solution.py:18
  116.0 2.5 %collective-permute-start.19 = (bf16[2,1024,128]{2,1,0:T(8,128)(2,1)}, bf16[2,1024,128]{2,1,0:T(8,128)(2,1)S(1)}, u32[]{:S(2)}, u32[]{:S(2)}) collective-permute-start(bf16[2,1024,128]{2,1,0:T(8,128)(2,1)} %copy-done.6), channel_id=1, source_target_pairs={{0,6},{1,7},{2,0},{3,1},{4,2},{5,3},{6,4},{7,5},{8,14},{9,15},{10,... | collective-permute-start | bytes 1572872 | tf_op jit(solution)/shard_map/ppermute | solution.py:18
  118.6 17.7 %all-to-all-done = bf16[8,12,32,128]{3,2,1,0:T(8,128)(2,1)} async-done(((bf16[8,12,32,128]{3,2,1,0:T(8,128)(2,1)}), bf16[8,12,32,128]{3,2,1,0:T(8,128)(2,1)}, u32[]{:S(2)}, u32[]{:S(2)}) %all-to-all-start) | async-done | bytes 786464 | tf_op jit(solution)/shard_map/all_to_all | solution.py:446
  136.3 1.3 convert_reduce_fusion
  137.5 1.9 %collective-permute-start.20 = (bf16[12,32,128]{2,1,0:T(8,128)(2,1)S(1)}, bf16[12,32,128]{2,1,0:T(8,128)(2,1)S(1)}, u32[]{:S(2)}, u32[]{:S(2)}) collective-permute-start(bf16[12,32,128]{2,1,0:T(8,128)(2,1)S(1)} %multiply_convert_fusion), channel_id=1, source_target_pairs={{1,32},{3,34},{5,36},{7,38},{9,40},{11,42},{13,44},{15,46},{17,48}... | collective-permute-start | bytes 294920 | tf_op jit(solution)/shard_map/ppermute | solution.py:460
  139.5 2.5 %finish.1 = (bf16[1024,128]{1,0:T(8,128)(2,1)}, bf16[1024,128]{1,0:T(8,128)(2,1)}) custom-call(bf16[1024,128]{1,0:T(8,128)(2,1)S(1)} %bitcast.31, bf16[1024,128]{1,0:T(8,128)(2,1)S(1)} %bitcast.37, f32[1024,128]{1,0:T(8,128)S(1)} %get-tuple-element.43.own_back, f32[1024,128]{1,0:T(8,128)S(1)} %get-tuple-element.44.own_ahead, ...), custom_call_target="tpu_custom_call" | custom-call | flops 10000000 | bytes 3670016 | tf_op jit(solution)/shard_map/finish/pallas_call | solution.py:37
  142.1 6.5 %collective-permute-done.20 = bf16[12,32,128]{2,1,0:T(8,128)(2,1)S(1)} collective-permute-done((bf16[12,32,128]{2,1,0:T(8,128)(2,1)S(1)}, bf16[12,32,128]{2,1,0:T(8,128)(2,1)S(1)}, u32[]{:S(2)}, u32[]{:S(2)}) %collective-permute-start.20) | collective-permute-done | bytes 98336 | tf_op jit(solution)/shard_map/ppermute | solution.py:460
  148.5 0.6 slice.44
  149.2 0.6 slice_bitcast_fusion
  (36 shorter events, 1.1 us)
Async XLA Ops:
  0.7 1.7 %copy-start = (bf16[3,3,1024,128]{3,2,1,0:T(8,128)(2,1)S(1)}, bf16[3,3,1024,128]{3,2,1,0:T(8,128)(2,1)}, u32[]{:S(2)}) copy-start(bf16[3,3,1024,128]{3,2,1,0:T(8,128)(2,1)} %param.6) | copy-start | bytes 7077892
  2.4 1.2 copy-start.3
  2.4 7.0 %copy-start.4 = (bf16[3,128,1024]{2,1,0:T(8,128)(2,1)S(1)}, bf16[3,128,1024]{2,1,0:T(8,128)(2,1)}, u32[]{:S(2)}) copy-start(bf16[3,128,1024]{2,1,0:T(8,128)(2,1)} %temporal.1) | copy-start | bytes 2359300
  2.4 20.4 %copy-start.5 = (bf16[1,8,8,16,128]{4,3,2,1,0:T(8,128)(2,1)S(1)}, bf16[1,8,8,16,128]{4,3,2,1,0:T(8,128)(2,1)}, u32[]{:S(2)}) copy-start(bf16[1,8,8,16,128]{4,3,2,1,0:T(8,128)(2,1)} %param.5) | copy-start | bytes 786436
  3.0 25.6 %copy-start.1 = (bf16[3,3,1024,128]{3,2,1,0:T(8,128)(2,1)S(1)}, bf16[3,3,1024,128]{3,2,1,0:T(8,128)(2,1)}, u32[]{:S(2)}) copy-start(bf16[3,3,1024,128]{3,2,1,0:T(8,128)(2,1)} %param.6) | copy-start | bytes 7077892
  3.0 17.1 %collective-permute-start = (bf16[9,2,128,128]{3,2,1,0:T(8,128)(2,1)S(1)}, bf16[9,2,128,128]{3,2,1,0:T(8,128)(2,1)S(1)}, u32[]{:S(2)}, u32[]{:S(2)}) collective-permute-start(bf16[9,2,128,128]{3,2,1,0:T(8,128)(2,1)S(1)} %spatial_give.1.after), channel_id=1, source_target_pairs={{0,129},{1,128},{2,131},{3,130},{4,133},{5,132},{6,135},{7,134},{8... | collective-permute-start | bytes 1769480 | tf_op jit(solution)/shard_map/ppermute | solution.py:341
  4.4 9.5 %collective-permute-start.1 = (bf16[1024,128]{1,0:T(8,128)(2,1)S(1)}, bf16[1024,128]{1,0:T(8,128)(2,1)S(1)}, u32[]{:S(2)}, u32[]{:S(2)}) collective-permute-start(bf16[1024,128]{1,0:T(8,128)(2,1)S(1)} %first_act.1.after.h0), channel_id=1, source_target_pairs={{0,2},{1,3},{2,4},{3,5},{4,6},{5,7},{6,0},{7,1},{8,10},{9,11},{10,... | collective-permute-start | bytes 786440 | tf_op jit(solution)/shard_map/ppermute | solution.py:18
  6.1 10.7 %collective-permute-start.2 = (bf16[1024,128]{1,0:T(8,128)(2,1)S(1)}, bf16[1024,128]{1,0:T(8,128)(2,1)S(1)}, u32[]{:S(2)}, u32[]{:S(2)}) collective-permute-start(bf16[1024,128]{1,0:T(8,128)(2,1)S(1)} %first_act.1.after.h0), channel_id=1, source_target_pairs={{0,4},{1,5},{2,6},{3,7},{4,0},{5,1},{6,2},{7,3},{8,12},{9,13},{10,... | collective-permute-start | bytes 786440 | tf_op jit(solution)/shard_map/ppermute | solution.py:18
  8.8 11.3 %collective-permute-start.3 = (bf16[1024,128]{1,0:T(8,128)(2,1)S(1)}, bf16[1024,128]{1,0:T(8,128)(2,1)S(1)}, u32[]{:S(2)}, u32[]{:S(2)}) collective-permute-start(bf16[1024,128]{1,0:T(8,128)(2,1)S(1)} %first_act.1.after.h0), channel_id=1, source_target_pairs={{0,6},{1,7},{2,0},{3,1},{4,2},{5,3},{6,4},{7,5},{8,14},{9,15},{10,... | collective-permute-start | bytes 786440 | tf_op jit(solution)/shard_map/ppermute | solution.py:18
  20.1 8.5 %collective-permute-start.4 = (bf16[9,2,128,128]{3,2,1,0:T(8,128)(2,1)S(1)}, bf16[9,2,128,128]{3,2,1,0:T(8,128)(2,1)S(1)}, u32[]{:S(2)}, u32[]{:S(2)}) collective-permute-start(bf16[9,2,128,128]{3,2,1,0:T(8,128)(2,1)S(1)} %collective-permute-done.got_a), channel_id=1, source_target_pairs={{0,8},{8,0},{16,24},{24,16},{32,40},{40,32},{48,56},{56,48},{64,72... | collective-permute-start | bytes 1769480 | tf_op jit(solution)/shard_map/ppermute | solution.py:22
  20.1 8.5 %collective-permute-start.9 = (bf16[3,2,128,128]{3,2,1,0:T(8,128)(2,1)S(1)}, bf16[3,2,128,128]{3,2,1,0:T(8,128)(2,1)S(1)}, u32[]{:S(2)}, u32[]{:S(2)}) collective-permute-start(bf16[3,2,128,128]{3,2,1,0:T(8,128)(2,1)S(1)} %temporal_give.1), channel_id=1, source_target_pairs={{0,129},{1,128},{2,131},{3,130},{4,133},{5,132},{6,135},{7,134},{8... | collective-permute-start | bytes 589832 | tf_op jit(solution)/shard_map/ppermute | solution.py:357
  22.8 12.2 %collective-permute-start.6 = (bf16[1024,128]{1,0:T(8,128)(2,1)S(1)}, bf16[1024,128]{1,0:T(8,128)(2,1)S(1)}, u32[]{:S(2)}, u32[]{:S(2)}) collective-permute-start(bf16[1024,128]{1,0:T(8,128)(2,1)S(1)} %bitcast.32), channel_id=1, source_target_pairs={{0,2},{1,3},{2,4},{3,5},{4,6},{5,7},{6,0},{7,1},{8,10},{9,11},{10,... | collective-permute-start | bytes 786440 | tf_op jit(solution)/shard_map/ppermute | solution.py:18
  24.1 10.9 %collective-permute-start.7 = (bf16[1024,128]{1,0:T(8,128)(2,1)S(1)}, bf16[1024,128]{1,0:T(8,128)(2,1)S(1)}, u32[]{:S(2)}, u32[]{:S(2)}) collective-permute-start(bf16[1024,128]{1,0:T(8,128)(2,1)S(1)} %bitcast.33), channel_id=1, source_target_pairs={{0,4},{1,5},{2,6},{3,7},{4,0},{5,1},{6,2},{7,3},{8,12},{9,13},{10,... | collective-permute-start | bytes 786440 | tf_op jit(solution)/shard_map/ppermute | solution.py:18
  25.7 13.4 %collective-permute-start.8 = (bf16[1024,128]{1,0:T(8,128)(2,1)S(1)}, bf16[1024,128]{1,0:T(8,128)(2,1)S(1)}, u32[]{:S(2)}, u32[]{:S(2)}) collective-permute-start(bf16[1024,128]{1,0:T(8,128)(2,1)S(1)} %bitcast.34), channel_id=1, source_target_pairs={{0,6},{1,7},{2,0},{3,1},{4,2},{5,3},{6,4},{7,5},{8,14},{9,15},{10,... | collective-permute-start | bytes 786440 | tf_op jit(solution)/shard_map/ppermute | solution.py:18
  28.6 10.6 %collective-permute-start.10 = (bf16[3,2,128,128]{3,2,1,0:T(8,128)(2,1)S(1)}, bf16[3,2,128,128]{3,2,1,0:T(8,128)(2,1)S(1)}, u32[]{:S(2)}, u32[]{:S(2)}) collective-permute-start(bf16[3,2,128,128]{3,2,1,0:T(8,128)(2,1)S(1)} %collective-permute-done.9.got_a), channel_id=1, source_target_pairs={{0,8},{8,0},{16,24},{24,16},{32,40},{40,32},{48,56},{56,48},{64,72... | collective-permute-start | bytes 589832 | tf_op jit(solution)/shard_map/ppermute | solution.py:22
  29.6 5.4 %copy-start.2 = (bf16[4608,256]{1,0:T(8,128)(2,1)}, bf16[4608,256]{1,0:T(8,128)(2,1)S(1)}, u32[]{:S(2)}) copy-start(bf16[4608,256]{1,0:T(8,128)(2,1)S(1)} %spatial_pair.1.pair.spatial) | copy-start | bytes 7077892
  42.0 10.8 %collective-permute-start.11 = (bf16[1024,128]{1,0:T(8,128)(2,1)S(1)}, bf16[1024,128]{1,0:T(8,128)(2,1)S(1)}, u32[]{:S(2)}, u32[]{:S(2)}) collective-permute-start(bf16[1024,128]{1,0:T(8,128)(2,1)S(1)} %get-tuple-element.40), channel_id=1, source_target_pairs={{0,1},{1,0},{2,3},{3,2},{4,5},{5,4},{6,7},{7,6},{8,9},{9,8},{10,11... | collective-permute-start | bytes 786440 | tf_op jit(solution)/shard_map/ppermute | solution.py:18
  42.3 15.0 %collective-permute-start.5 = (bf16[1024,128]{1,0:T(8,128)(2,1)S(1)}, bf16[1024,128]{1,0:T(8,128)(2,1)S(1)}, u32[]{:S(2)}, u32[]{:S(2)}) collective-permute-start(bf16[1024,128]{1,0:T(8,128)(2,1)S(1)} %get-tuple-element.37.after), channel_id=1, source_target_pairs={{0,1},{1,0},{2,3},{3,2},{4,5},{5,4},{6,7},{7,6},{8,9},{9,8},{10,11... | collective-permute-start | bytes 786440 | tf_op jit(solution)/shard_map/ppermute | solution.py:18
  58.7 14.3 %collective-permute-start.12 = (bf16[2,1024,128]{2,1,0:T(8,128)(2,1)S(1)}, bf16[2,1024,128]{2,1,0:T(8,128)(2,1)S(1)}, u32[]{:S(2)}, u32[]{:S(2)}) collective-permute-start(bf16[2,1024,128]{2,1,0:T(8,128)(2,1)S(1)} %second_act.1.b0), channel_id=1, source_target_pairs={{0,1},{1,0},{2,3},{3,2},{4,5},{5,4},{6,7},{7,6},{8,9},{9,8},{10,11... | collective-permute-start | bytes 1572872 | tf_op jit(solution)/shard_map/ppermute | solution.py:18
  77.5 6.5 %collective-permute-start.13 = (bf16[2,8,6,32,128]{4,3,2,1,0:T(8,128)(2,1)S(1)}, bf16[2,8,6,32,128]{4,3,2,1,0:T(8,128)(2,1)S(1)}, u32[]{:S(2)}, u32[]{:S(2)}) collective-permute-start(bf16[2,8,6,32,128]{4,3,2,1,0:T(8,128)(2,1)S(1)} %get-tuple-element.41.after), channel_id=1, source_target_pairs={{0,8},{8,0},{16,24},{24,16},{32,40},{40,32},{48,56},{56,48},{64,72... | collective-permute-start | bytes 2359304 | tf_op jit(solution)/shard_map/ppermute | solution.py:22
  83.6 2.4 %collective-permute-start.15 = (bf16[2,8,6,32,128]{4,3,2,1,0:T(8,128)(2,1)S(1)}, bf16[2,8,6,32,128]{4,3,2,1,0:T(8,128)(2,1)S(1)}, u32[]{:S(2)}, u32[]{:S(2)}) collective-permute-start(bf16[2,8,6,32,128]{4,3,2,1,0:T(8,128)(2,1)S(1)} %get-tuple-element.42.after), channel_id=1, source_target_pairs={{0,8},{8,0},{16,24},{24,16},{32,40},{40,32},{48,56},{56,48},{64,72... | collective-permute-start | bytes 2359304 | tf_op jit(solution)/shard_map/ppermute | solution.py:22
  84.5 1.7 %copy-start.7 = (f32[2,8,6,32,128]{4,3,2,1,0:T(8,128)S(1)}, f32[2,8,6,32,128]{4,3,2,1,0:T(8,128)}, u32[]{:S(2)}) copy-start(f32[2,8,6,32,128]{4,3,2,1,0:T(8,128)} %get-tuple-element.46) | copy-start | bytes 4718596
  84.5 12.1 %collective-permute-start.14 = (bf16[8,6,32,128]{3,2,1,0:T(8,128)(2,1)S(1)}, bf16[8,6,32,128]{3,2,1,0:T(8,128)(2,1)S(1)}, u32[]{:S(2)}, u32[]{:S(2)}) collective-permute-start(bf16[8,6,32,128]{3,2,1,0:T(8,128)(2,1)S(1)} %fusion.8), channel_id=1, source_target_pairs={{0,128},{8,136},{16,144},{24,152},{32,160},{40,168},{48,176},{56,1... | collective-permute-start | bytes 1179656 | tf_op jit(solution)/shard_map/ppermute | solution.py:22
  86.4 17.6 %collective-permute-start.16 = (bf16[8,6,32,128]{3,2,1,0:T(8,128)(2,1)S(1)}, bf16[8,6,32,128]{3,2,1,0:T(8,128)(2,1)S(1)}, u32[]{:S(2)}, u32[]{:S(2)}) collective-permute-start(bf16[8,6,32,128]{3,2,1,0:T(8,128)(2,1)S(1)} %fusion.9), channel_id=1, source_target_pairs={{0,128},{8,136},{16,144},{24,152},{32,160},{40,168},{48,176},{56,1... | collective-permute-start | bytes 1179656 | tf_op jit(solution)/shard_map/ppermute | solution.py:22
  95.5 8.8 %copy-start.6 = (bf16[2,1024,128]{2,1,0:T(8,128)(2,1)}, bf16[2,1024,128]{2,1,0:T(8,128)(2,1)S(1)}, u32[]{:S(2)}) copy-start(bf16[2,1024,128]{2,1,0:T(8,128)(2,1)S(1)} %get-tuple-element.52) | copy-start | bytes 1572868
  105.2 31.0 %all-to-all-start = ((bf16[8,12,32,128]{3,2,1,0:T(8,128)(2,1)}), bf16[8,12,32,128]{3,2,1,0:T(8,128)(2,1)}, u32[]{:S(2)}, u32[]{:S(2)}) async-start(bf16[8,12,32,128]{3,2,1,0:T(8,128)(2,1)} %pad_maximum_fusion), calls=%async_computation | async-start | bytes 1572864 | tf_op jit(solution)/shard_map/all_to_all | solution.py:446
  113.7 25.8 %collective-permute-start.17 = (bf16[2,1024,128]{2,1,0:T(8,128)(2,1)}, bf16[2,1024,128]{2,1,0:T(8,128)(2,1)S(1)}, u32[]{:S(2)}, u32[]{:S(2)}) collective-permute-start(bf16[2,1024,128]{2,1,0:T(8,128)(2,1)} %get-tuple-element.50), channel_id=1, source_target_pairs={{0,2},{1,3},{2,4},{3,5},{4,6},{5,7},{6,0},{7,1},{8,10},{9,11},{10,... | collective-permute-start | bytes 1572872 | tf_op jit(solution)/shard_map/ppermute | solution.py:18
  113.7 25.8 %collective-permute-start.18 = (bf16[2,1024,128]{2,1,0:T(8,128)(2,1)}, bf16[2,1024,128]{2,1,0:T(8,128)(2,1)S(1)}, u32[]{:S(2)}, u32[]{:S(2)}) collective-permute-start(bf16[2,1024,128]{2,1,0:T(8,128)(2,1)} %get-tuple-element.51), channel_id=1, source_target_pairs={{0,4},{1,5},{2,6},{3,7},{4,0},{5,1},{6,2},{7,3},{8,12},{9,13},{10,... | collective-permute-start | bytes 1572872 | tf_op jit(solution)/shard_map/ppermute | solution.py:18
  116.0 23.5 %collective-permute-start.19 = (bf16[2,1024,128]{2,1,0:T(8,128)(2,1)}, bf16[2,1024,128]{2,1,0:T(8,128)(2,1)S(1)}, u32[]{:S(2)}, u32[]{:S(2)}) collective-permute-start(bf16[2,1024,128]{2,1,0:T(8,128)(2,1)} %copy-done.6), channel_id=1, source_target_pairs={{0,6},{1,7},{2,0},{3,1},{4,2},{5,3},{6,4},{7,5},{8,14},{9,15},{10,... | collective-permute-start | bytes 1572872 | tf_op jit(solution)/shard_map/ppermute | solution.py:18
  137.5 11.0 %collective-permute-start.20 = (bf16[12,32,128]{2,1,0:T(8,128)(2,1)S(1)}, bf16[12,32,128]{2,1,0:T(8,128)(2,1)S(1)}, u32[]{:S(2)}, u32[]{:S(2)}) collective-permute-start(bf16[12,32,128]{2,1,0:T(8,128)(2,1)S(1)} %multiply_convert_fusion), channel_id=1, source_target_pairs={{1,32},{3,34},{5,36},{7,38},{9,40},{11,42},{13,44},{15,46},{17,48}... | collective-permute-start | bytes 294920 | tf_op jit(solution)/shard_map/ppermute | solution.py:460

commit v3 on v2

--- a/solution.py
+++ b/solution.py
@@ -161,7 +161,7 @@
             give[k, j] = weight[k, :, at]
 
 
-def spatial_pair_kernel(place, weight, got_a, got_b, pair):
+def spatial_pair_kernel(place, weight, got_a, got_b, after, pair):
     x_hi, core = place[1], place[2]
     for tap in range(9):
         for yb in range(4):
@@ -195,21 +195,36 @@
     lax.fori_loop(0, 4, step, 0)
 
 
-def spatial_out_kernel(place, h0, h1, h2, h3, pair, own, give, wide):
-    y = place[0]
-    for d, piece in enumerate((h0, h1, h2, h3)):
+def spatial_product(y, pieces, half, wide, result):
+    for d, piece in enumerate(pieces):
         yb = lax.rem(y - d + 4, 4)
         unfold(piece[...], wide, lambda sa, sb: block(((sa + 1) * 3 + sb + 1) * 4 + yb))
 
     def step(i, carry):
         rows = pl.ds(pl.multiple_of(i * 256, 256), 256)
         left = wide[pl.ds(2 * i, 2)].reshape(256, 4608)
-        total = jnp.dot(left, pair[...], preferred_element_type=F32)
-        own[rows, :] = total[:, :128]
-        give[rows, :] = total[:, 128:].astype(BF)
+        result[rows, :] = jnp.dot(left, half[...], preferred_element_type=F32).astype(result.dtype)
         return carry
 
     lax.fori_loop(0, 4, step, 0)
+
+
+def spatial_partner_kernel(place, h0, h1, h2, h3, got_a, got_b, give, half, wide):
+    core = place[2]
+    for tap in range(9):
+        for j in range(2):
+            half[block(tap * 4 + 2 * core + j), :] = got_a[tap, j]
+            half[block(tap * 4 + 2 - 2 * core + j), :] = got_b[tap, j]
+    spatial_product(place[0], (h0, h1, h2, h3), half, wide, give)
+
+
+def spatial_own_kernel(place, h0, h1, h2, h3, weight, after, own, half, wide):
+    x_hi = place[1]
+    for tap in range(9):
+        for yb in range(4):
+            at = tap * 512 + yb * 128
+            half[at : at + 128, :] = weight[tap, block(2 * yb + x_hi), :]
+    spatial_product(place[0], (h0, h1, h2, h3), half, wide, own)
 
 
 def both_back_kernel(
@@ -283,7 +298,7 @@
     lax.fori_loop(0, taps, step, 0)
 
 
-def early_grads_kernel(place, h0, h1, h2, h3, b0, b1, keep, give, first, wide, total):
+def early_grads_kernel(place, h0, h1, h2, h3, b0, b1, after, keep, give, first, wide, total):
     transposed(place[0], (h0, h1, h2, h3), first)
     fill_grads((b0, b1), wide, (1, 0))
     spatial_taps(place, first, wide, keep, give, total, 6)
@@ -355,25 +370,37 @@
     spatial_b = data_move(spatial_a, 1)
     grads_all = [grads] + [tensor_move(grads, d, 0) for d in (1, 2, 3)]
     temporal_a = lax.ppermute(temporal_give, ("dp", "tensor"), cross)
+    out_scratch = [pltpu.VMEM((4608, 128), BF), pltpu.VMEM((8, 128, 4608), BF)]
+    (out_give,) = call(
+        spatial_partner_kernel,
+        [piece],
+        out_scratch,
+        [place] + first_all + [spatial_a, spatial_b],
+        ROWS * 4608 * 256,
+        "spatial_partner",
+    )
+    temporal_a, out_give = lax.optimization_barrier((temporal_a, out_give))
     temporal_b = data_move(temporal_a, 1)
     temporal_args = [temporal, temporal_a, temporal_b]
+    (out_own,) = call(
+        spatial_own_kernel,
+        [wide_piece],
+        out_scratch,
+        [place] + first_all + [spatial, out_give],
+        ROWS * 4608 * 256,
+        "spatial_own",
+        unread=1,
+    )
+    out_got = tensor_move(out_give, 0, 1)
     (spatial_pair,) = call(
         spatial_pair_kernel,
         [shape((4608, 256), BF)],
         [],
-        [place, spatial, spatial_a, spatial_b],
+        [place, spatial, spatial_a, spatial_b, out_give],
         10**6,
         "spatial_pair",
-    )
-    out_own, out_give = call(
-        spatial_out_kernel,
-        [wide_piece, piece],
-        [pltpu.VMEM((8, 128, 4608), BF)],
-        [place] + first_all + [spatial_pair],
-        2 * ROWS * 4608 * 256,
-        "spatial_out",
-    )
-    out_got = tensor_move(out_give, 0, 1)
+        unread=1,
+    )
     second_own, second_give = call(
         grad_second_kernel,
         [wide_piece, piece],
@@ -403,9 +430,10 @@
             pltpu.VMEM((8, 128, 1536), BF),
             pltpu.VMEM((512, 256), F32),
         ],
-        [place] + first_all + both_pair,
+        [place] + first_all + both_pair + [spatial_pair],
         2 * ROWS * 1536 * 512,
         "early_grads",
+        unread=1,
     )
     late_keep, late_give = call(
         late_grads_kernel,

time: 150 us -> 145 us (0.967)
  waiting for transfers between devices: 75.1 us -> 65.4 us
  Pallas kernels: 34 us -> 39.4 us
  starting transfers between devices: 33.3 us -> 30.7 us
    ppermute x12, waiting for transfers between devices: 39.8 us -> 31.6 us  [tensor_move(): return lax.ppermute(values, 'tensor', pairs)]
    pallas_call x11 -> x12, Pallas kernels: 34 us -> 39.4 us  [call(): pl.pallas_call(body, out_shape=outs, in_specs=specs, out_specs=[vmem] * l...]
    ppermute x12, starting transfers between devices: 18.3 us -> 15.4 us  [tensor_move(): return lax.ppermute(values, 'tensor', pairs)]
  transfers between devices with their start and end apart: 22 -> 22, of which waited for: 13 -> 12; matrix products, arithmetic and copies ran while one was open for 1% -> 2% of each run, Pallas kernels for 16% -> 23%
where the time goes in v3:
time: 145 us; the launch traced here: 144 us
  waiting for transfers between devices  65.4 us (45%)
  Pallas kernels  39.4 us (27%)
  starting transfers between devices  30.7 us (21%)
  local copies, waits for them, and re-layouts  4.35 us (3%)
  other arithmetic  3.55 us (2%)
    pallas_call x12, Pallas kernels, call(): pl.pallas_call(body, out_shape=outs, in_specs=specs, out_specs=[vmem] * l...  39.4 us
    ppermute x12, waiting for transfers between devices, tensor_move(): return lax.ppermute(values, 'tensor', pairs)  31.6 us
    all_to_all x1, waiting for transfers between devices, per_device(): lax.all_to_all(local, 'dp', split_axis=0, concat_axis=0, tiled=True, axis...  17.7 us
    ppermute x12, starting transfers between devices, tensor_move(): return lax.ppermute(values, 'tensor', pairs)  15.4 us
    ppermute x6, waiting for transfers between devices, data_move(): return lax.ppermute(values, 'dp', [(d, d ^ bits) for d in range(32)])  9.54 us
    all_to_all x1, starting transfers between devices, per_device(): lax.all_to_all(local, 'dp', split_axis=0, concat_axis=0, tiled=True, axis...  8.51 us
    ppermute x1, waiting for transfers between devices, per_device(): moved = lax.ppermute(share, ('dp', 'tensor'), move)  6.46 us
    unnamed x16, local copies, waits for them, and re-layouts  3.1 us
  transfers between devices with their start and end apart: 22, of which 12 were waited for; matrix products, arithmetic and copies ran while one was open for 2% of the time, Pallas kernels for 23%

profile of v3, /device:TPU:14, one launch (start us, length us, event | category | flops | bytes accessed | tf_op | source)
XLA Modules:
  0.0 144.4 jit_solution(15341954888635579745)
XLA Ops:
  0.7 1.7 %copy-done = bf16[3,3,1024,128]{3,2,1,0:T(8,128)(2,1)S(1)} copy-done((bf16[3,3,1024,128]{3,2,1,0:T(8,128)(2,1)S(1)}, bf16[3,3,1024,128]{3,2,1,0:T(8,128)(2,1)}, u32[]{:S(2)}) %copy-start) | copy-done | bytes 2359320
  2.4 0.6 spatial_give.1.after
  3.0 0.6 collective-permute-start
  3.6 0.8 first_act.1.after.h0
  4.4 1.7 %collective-permute-start.1 = (bf16[1024,128]{1,0:T(8,128)(2,1)S(1)}, bf16[1024,128]{1,0:T(8,128)(2,1)S(1)}, u32[]{:S(2)}, u32[]{:S(2)}) collective-permute-start(bf16[1024,128]{1,0:T(8,128)(2,1)S(1)} %first_act.1.after.h0), channel_id=1, source_target_pairs={{0,2},{1,3},{2,4},{3,5},{4,6},{5,7},{6,0},{7,1},{8,10},{9,11},{10,... | collective-permute-start | bytes 786440 | tf_op jit(solution)/shard_map/ppermute | solution.py:18
  6.1 2.7 %collective-permute-start.2 = (bf16[1024,128]{1,0:T(8,128)(2,1)S(1)}, bf16[1024,128]{1,0:T(8,128)(2,1)S(1)}, u32[]{:S(2)}, u32[]{:S(2)}) collective-permute-start(bf16[1024,128]{1,0:T(8,128)(2,1)S(1)} %first_act.1.after.h0), channel_id=1, source_target_pairs={{0,4},{1,5},{2,6},{3,7},{4,0},{5,1},{6,2},{7,3},{8,12},{9,13},{10,... | collective-permute-start | bytes 786440 | tf_op jit(solution)/shard_map/ppermute | solution.py:18
  8.8 0.7 collective-permute-start.3
  9.5 0.6 temporal_give.1
  10.1 3.9 %collective-permute-done.1.h1 = bf16[1024,128]{1,0:T(8,128)(2,1)S(1)} collective-permute-done((bf16[1024,128]{1,0:T(8,128)(2,1)S(1)}, bf16[1024,128]{1,0:T(8,128)(2,1)S(1)}, u32[]{:S(2)}, u32[]{:S(2)}) %collective-permute-start.1) | collective-permute-done | bytes 262176 | tf_op jit(solution)/shard_map/ppermute | solution.py:18
  13.9 2.9 %collective-permute-done.2.h2 = bf16[1024,128]{1,0:T(8,128)(2,1)S(1)} collective-permute-done((bf16[1024,128]{1,0:T(8,128)(2,1)S(1)}, bf16[1024,128]{1,0:T(8,128)(2,1)S(1)}, u32[]{:S(2)}, u32[]{:S(2)}) %collective-permute-start.2) | collective-permute-done | bytes 262176 | tf_op jit(solution)/shard_map/ppermute | solution.py:18
  16.9 3.2 %collective-permute-done.3.h3 = bf16[1024,128]{1,0:T(8,128)(2,1)S(1)} collective-permute-done((bf16[1024,128]{1,0:T(8,128)(2,1)S(1)}, bf16[1024,128]{1,0:T(8,128)(2,1)S(1)}, u32[]{:S(2)}, u32[]{:S(2)}) %collective-permute-start.3) | collective-permute-done | bytes 262176 | tf_op jit(solution)/shard_map/ppermute | solution.py:18
  20.1 2.7 %collective-permute-start.4 = (bf16[3,2,128,128]{3,2,1,0:T(8,128)(2,1)S(1)}, bf16[3,2,128,128]{3,2,1,0:T(8,128)(2,1)S(1)}, u32[]{:S(2)}, u32[]{:S(2)}) collective-permute-start(bf16[3,2,128,128]{3,2,1,0:T(8,128)(2,1)S(1)} %temporal_give.1), channel_id=1, source_target_pairs={{0,129},{1,128},{2,131},{3,130},{4,133},{5,132},{6,135},{7,134},{8... | collective-permute-start | bytes 589832 | tf_op jit(solution)/shard_map/ppermute | solution.py:372
  22.8 1.3 collective-permute-start.7
  24.1 1.7 %collective-permute-start.8 = (bf16[1024,128]{1,0:T(8,128)(2,1)S(1)}, bf16[1024,128]{1,0:T(8,128)(2,1)S(1)}, u32[]{:S(2)}, u32[]{:S(2)}) collective-permute-start(bf16[1024,128]{1,0:T(8,128)(2,1)S(1)} %bitcast.34), channel_id=1, source_target_pairs={{0,4},{1,5},{2,6},{3,7},{4,0},{5,1},{6,2},{7,3},{8,12},{9,13},{10,... | collective-permute-start | bytes 786440 | tf_op jit(solution)/shard_map/ppermute | solution.py:18
  25.7 1.5 %collective-permute-start.9 = (bf16[1024,128]{1,0:T(8,128)(2,1)S(1)}, bf16[1024,128]{1,0:T(8,128)(2,1)S(1)}, u32[]{:S(2)}, u32[]{:S(2)}) collective-permute-start(bf16[1024,128]{1,0:T(8,128)(2,1)S(1)} %bitcast.35), channel_id=1, source_target_pairs={{0,6},{1,7},{2,0},{3,1},{4,2},{5,3},{6,4},{7,5},{8,14},{9,15},{10,... | collective-permute-start | bytes 786440 | tf_op jit(solution)/shard_map/ppermute | solution.py:18
  27.2 5.4 %spatial_partner.1.after = bf16[1024,128]{1,0:T(8,128)(2,1)S(1)} custom-call(s32[4]{0:T(128)S(1)} %pad_add_fusion.place, bf16[1024,128]{1,0:T(8,128)(2,1)S(1)} %first_act.1.after.h0, bf16[1024,128]{1,0:T(8,128)(2,1)S(1)} %collective-permute-done.1.h1, bf16[1024,128]{1,0:T(8,128)(2,1)S(1)} %collective-permute-done.2.h2, ...), custom_call_target="tpu_custom_call" | custom-call | flops 1207959552 | bytes 2490384 | tf_op jit(solution)/shard_map/spatial_partner/pallas_call | solution.py:37
  32.7 0.3 collective-permute-start.6
  33.0 1.7 %collective-permute-done.8.g2 = bf16[1024,128]{1,0:T(8,128)(2,1)S(1)} collective-permute-done((bf16[1024,128]{1,0:T(8,128)(2,1)S(1)}, bf16[1024,128]{1,0:T(8,128)(2,1)S(1)}, u32[]{:S(2)}, u32[]{:S(2)}) %collective-permute-start.8) | collective-permute-done | bytes 262176 | tf_op jit(solution)/shard_map/ppermute | solution.py:18
  34.8 4.4 %collective-permute-done.9.g3 = bf16[1024,128]{1,0:T(8,128)(2,1)S(1)} collective-permute-done((bf16[1024,128]{1,0:T(8,128)(2,1)S(1)}, bf16[1024,128]{1,0:T(8,128)(2,1)S(1)}, u32[]{:S(2)}, u32[]{:S(2)}) %collective-permute-start.9) | collective-permute-done | bytes 262176 | tf_op jit(solution)/shard_map/ppermute | solution.py:18
  39.2 2.8 %grad_second.1 = (f32[1024,128]{1,0:T(8,128)S(1)}, bf16[1024,128]{1,0:T(8,128)(2,1)S(1)}) custom-call(s32[4]{0:T(128)S(1)} %pad_add_fusion.place, bf16[1024,128]{1,0:T(8,128)(2,1)S(1)} %bitcast.36, bf16[1024,128]{1,0:T(8,128)(2,1)S(1)} %collective-permute-done.7.g1, bf16[1024,128]{1,0:T(8,128)(2,1)S(1)} %collective-permute-done.8.g2, ...), custom_call_target="tpu_custom_call" | custom-call | flops 805306368 | bytes 3276816 | tf_op jit(solution)/shard_map/grad_second/pallas_call | solution.py:37
  42.0 0.4 collective-permute-start.11
  42.4 5.4 %spatial_own.1.out_own = f32[1024,128]{1,0:T(8,128)S(1)} custom-call(s32[4]{0:T(128)S(1)} %pad_add_fusion.place, bf16[1024,128]{1,0:T(8,128)(2,1)S(1)} %first_act.1.after.h0, bf16[1024,128]{1,0:T(8,128)(2,1)S(1)} %collective-permute-done.1.h1, bf16[1024,128]{1,0:T(8,128)(2,1)S(1)} %collective-permute-done.2.h2, ...), custom_call_target="tpu_custom_call" | custom-call | flops 1207959552 | bytes 4194320 | tf_op jit(solution)/shard_map/spatial_own/pallas_call | solution.py:37
  47.8 3.9 %collective-permute-done.11.grad_got = bf16[1024,128]{1,0:T(8,128)(2,1)S(1)} collective-permute-done((bf16[1024,128]{1,0:T(8,128)(2,1)S(1)}, bf16[1024,128]{1,0:T(8,128)(2,1)S(1)}, u32[]{:S(2)}, u32[]{:S(2)}) %collective-permute-start.11) | collective-permute-done | bytes 262176 | tf_op jit(solution)/shard_map/ppermute | solution.py:18
  51.8 1.4 second_act.1.b0
  53.2 0.4 collective-permute-start.12
  53.6 1.0 spatial_pair.1.after.spatial
  54.6 1.4 copy-done.2
  56.0 11.6 %collective-permute-done.12.b1 = bf16[2,1024,128]{2,1,0:T(8,128)(2,1)S(1)} collective-permute-done((bf16[2,1024,128]{2,1,0:T(8,128)(2,1)S(1)}, bf16[2,1024,128]{2,1,0:T(8,128)(2,1)S(1)}, u32[]{:S(2)}, u32[]{:S(2)}) %collective-permute-start.12) | collective-permute-done | bytes 524320 | tf_op jit(solution)/shard_map/ppermute | solution.py:18
  67.5 4.5 %early_grads.1 = (f32[2,8,6,32,128]{4,3,2,1,0:T(8,128)S(1)}, bf16[2,8,6,32,128]{4,3,2,1,0:T(8,128)(2,1)S(1)}) custom-call(s32[4]{0:T(128)S(1)} %pad_add_fusion.place, bf16[1024,128]{1,0:T(8,128)(2,1)S(1)} %first_act.1.after.h0, bf16[1024,128]{1,0:T(8,128)(2,1)S(1)} %collective-permute-done.1.h1, bf16[1024,128]{1,0:T(8,128)(2,1)S(1)} %collective-permute-done.2.h2, ...), custom_call_target="tpu_custom_call" | custom-call | flops 1610612736 | bytes 6815760 | tf_op jit(solution)/shard_map/early_grads/pallas_call | solution.py:37
  72.2 5.9 %late_grads.1 = (f32[2,8,6,32,128]{4,3,2,1,0:T(8,128)}, bf16[2,8,6,32,128]{4,3,2,1,0:T(8,128)(2,1)S(1)}) custom-call(s32[4]{0:T(128)S(1)} %pad_add_fusion.place, bf16[1024,128]{1,0:T(8,128)(2,1)S(1)} %first_act.1.after.h0, bf16[1024,128]{1,0:T(8,128)(2,1)S(1)} %collective-permute-done.1.h1, bf16[1024,128]{1,0:T(8,128)(2,1)S(1)} %collective-permute-done.2.h2, ...), custom_call_target="tpu_custom_call" | custom-call | flops 1610612736 | bytes 6291472 | tf_op jit(solution)/shard_map/late_grads/pallas_call | solution.py:37
  78.1 0.5 collective-permute-start.15
  79.1 1.4 collective-permute-done.15
  80.9 0.9 collective-permute-start.16
  81.8 8.4 %both_back.1 = (f32[1024,128]{1,0:T(8,128)S(1)}, f32[1024,128]{1,0:T(8,128)S(1)}, bf16[2,1024,128]{2,1,0:T(8,128)(2,1)}, bf16[2,1024,128]{2,1,0:T(8,128)(2,1)}, bf16[2,1024,128]{2,1,0:T(8,128)(2,1)S(1)}) custom-call(s32[4]{0:T(128)S(1)} %pad_add_fusion.place, bf16[2,1024,128]{2,1,0:T(8,128)(2,1)S(1)} %second_act.1.b0, ...), custom_call_target="tpu_custom_call" | custom-call | flops 3221225472 | bytes 7995408 | tf_op jit(solution)/shard_map/both_back/pallas_call | solution.py:37
  90.2 0.8 collective-permute-done.14
  91.3 7.3 %collective-permute-done.16 = bf16[8,6,32,128]{3,2,1,0:T(8,128)(2,1)S(1)} collective-permute-done((bf16[8,6,32,128]{3,2,1,0:T(8,128)(2,1)S(1)}, bf16[8,6,32,128]{3,2,1,0:T(8,128)(2,1)S(1)}, u32[]{:S(2)}, u32[]{:S(2)}) %collective-permute-start.16) | collective-permute-done | bytes 393248 | tf_op jit(solution)/shard_map/ppermute | solution.py:22
  98.5 0.2 fusion.3
  98.8 1.0 pad_maximum_fusion
  99.8 8.5 %all-to-all-start = ((bf16[8,12,32,128]{3,2,1,0:T(8,128)(2,1)}), bf16[8,12,32,128]{3,2,1,0:T(8,128)(2,1)}, u32[]{:S(2)}, u32[]{:S(2)}) async-start(bf16[8,12,32,128]{3,2,1,0:T(8,128)(2,1)} %pad_maximum_fusion), calls=%async_computation | async-start | bytes 1572864 | tf_op jit(solution)/shard_map/all_to_all | solution.py:474
  108.3 2.3 %collective-permute-start.18 = (bf16[2,1024,128]{2,1,0:T(8,128)(2,1)}, bf16[2,1024,128]{2,1,0:T(8,128)(2,1)S(1)}, u32[]{:S(2)}, u32[]{:S(2)}) collective-permute-start(bf16[2,1024,128]{2,1,0:T(8,128)(2,1)} %get-tuple-element.51), channel_id=1, source_target_pairs={{0,4},{1,5},{2,6},{3,7},{4,0},{5,1},{6,2},{7,3},{8,12},{9,13},{10,... | collective-permute-start | bytes 1572872 | tf_op jit(solution)/shard_map/ppermute | solution.py:18
  110.6 2.5 %collective-permute-start.19 = (bf16[2,1024,128]{2,1,0:T(8,128)(2,1)}, bf16[2,1024,128]{2,1,0:T(8,128)(2,1)S(1)}, u32[]{:S(2)}, u32[]{:S(2)}) collective-permute-start(bf16[2,1024,128]{2,1,0:T(8,128)(2,1)} %copy-done.6), channel_id=1, source_target_pairs={{0,6},{1,7},{2,0},{3,1},{4,2},{5,3},{6,4},{7,5},{8,14},{9,15},{10,... | collective-permute-start | bytes 1572872 | tf_op jit(solution)/shard_map/ppermute | solution.py:18
  113.1 17.7 %all-to-all-done = bf16[8,12,32,128]{3,2,1,0:T(8,128)(2,1)} async-done(((bf16[8,12,32,128]{3,2,1,0:T(8,128)(2,1)}), bf16[8,12,32,128]{3,2,1,0:T(8,128)(2,1)}, u32[]{:S(2)}, u32[]{:S(2)}) %all-to-all-start) | async-done | bytes 786464 | tf_op jit(solution)/shard_map/all_to_all | solution.py:474
  130.8 1.3 convert_reduce_fusion
  132.1 1.9 %collective-permute-start.20 = (bf16[12,32,128]{2,1,0:T(8,128)(2,1)S(1)}, bf16[12,32,128]{2,1,0:T(8,128)(2,1)S(1)}, u32[]{:S(2)}, u32[]{:S(2)}) collective-permute-start(bf16[12,32,128]{2,1,0:T(8,128)(2,1)S(1)} %multiply_convert_fusion), channel_id=1, source_target_pairs={{1,32},{3,34},{5,36},{7,38},{9,40},{11,42},{13,44},{15,46},{17,48}... | collective-permute-start | bytes 294920 | tf_op jit(solution)/shard_map/ppermute | solution.py:488
  134.1 2.5 %finish.1 = (bf16[1024,128]{1,0:T(8,128)(2,1)}, bf16[1024,128]{1,0:T(8,128)(2,1)}) custom-call(bf16[1024,128]{1,0:T(8,128)(2,1)S(1)} %bitcast.32, bf16[1024,128]{1,0:T(8,128)(2,1)S(1)} %bitcast.38, f32[1024,128]{1,0:T(8,128)S(1)} %get-tuple-element.43.own_back, f32[1024,128]{1,0:T(8,128)S(1)} %get-tuple-element.44.own_ahead, ...), custom_call_target="tpu_custom_call" | custom-call | flops 10000000 | bytes 3670016 | tf_op jit(solution)/shard_map/finish/pallas_call | solution.py:37
  136.6 6.5 %collective-permute-done.20 = bf16[12,32,128]{2,1,0:T(8,128)(2,1)S(1)} collective-permute-done((bf16[12,32,128]{2,1,0:T(8,128)(2,1)S(1)}, bf16[12,32,128]{2,1,0:T(8,128)(2,1)S(1)}, u32[]{:S(2)}, u32[]{:S(2)}) %collective-permute-start.20) | collective-permute-done | bytes 98336 | tf_op jit(solution)/shard_map/ppermute | solution.py:488
  143.1 0.6 slice.44
  143.8 0.6 slice_bitcast_fusion
  (37 shorter events, 1.4 us)
Async XLA Ops:
  0.7 1.7 %copy-start = (bf16[3,3,1024,128]{3,2,1,0:T(8,128)(2,1)S(1)}, bf16[3,3,1024,128]{3,2,1,0:T(8,128)(2,1)}, u32[]{:S(2)}) copy-start(bf16[3,3,1024,128]{3,2,1,0:T(8,128)(2,1)} %param.6) | copy-start | bytes 7077892
  2.4 1.2 copy-start.3
  2.4 7.0 %copy-start.4 = (bf16[3,128,1024]{2,1,0:T(8,128)(2,1)S(1)}, bf16[3,128,1024]{2,1,0:T(8,128)(2,1)}, u32[]{:S(2)}) copy-start(bf16[3,128,1024]{2,1,0:T(8,128)(2,1)} %temporal.1) | copy-start | bytes 2359300
  3.0 19.8 %copy-start.5 = (bf16[1,8,8,16,128]{4,3,2,1,0:T(8,128)(2,1)S(1)}, bf16[1,8,8,16,128]{4,3,2,1,0:T(8,128)(2,1)}, u32[]{:S(2)}) copy-start(bf16[1,8,8,16,128]{4,3,2,1,0:T(8,128)(2,1)} %param.5) | copy-start | bytes 786436
  3.0 17.1 %collective-permute-start = (bf16[9,2,128,128]{3,2,1,0:T(8,128)(2,1)S(1)}, bf16[9,2,128,128]{3,2,1,0:T(8,128)(2,1)S(1)}, u32[]{:S(2)}, u32[]{:S(2)}) collective-permute-start(bf16[9,2,128,128]{3,2,1,0:T(8,128)(2,1)S(1)} %spatial_give.1.after), channel_id=1, source_target_pairs={{0,129},{1,128},{2,131},{3,130},{4,133},{5,132},{6,135},{7,134},{8... | collective-permute-start | bytes 1769480 | tf_op jit(solution)/shard_map/ppermute | solution.py:356
  4.4 9.5 %collective-permute-start.1 = (bf16[1024,128]{1,0:T(8,128)(2,1)S(1)}, bf16[1024,128]{1,0:T(8,128)(2,1)S(1)}, u32[]{:S(2)}, u32[]{:S(2)}) collective-permute-start(bf16[1024,128]{1,0:T(8,128)(2,1)S(1)} %first_act.1.after.h0), channel_id=1, source_target_pairs={{0,2},{1,3},{2,4},{3,5},{4,6},{5,7},{6,0},{7,1},{8,10},{9,11},{10,... | collective-permute-start | bytes 786440 | tf_op jit(solution)/shard_map/ppermute | solution.py:18
  6.1 10.8 %collective-permute-start.2 = (bf16[1024,128]{1,0:T(8,128)(2,1)S(1)}, bf16[1024,128]{1,0:T(8,128)(2,1)S(1)}, u32[]{:S(2)}, u32[]{:S(2)}) collective-permute-start(bf16[1024,128]{1,0:T(8,128)(2,1)S(1)} %first_act.1.after.h0), channel_id=1, source_target_pairs={{0,4},{1,5},{2,6},{3,7},{4,0},{5,1},{6,2},{7,3},{8,12},{9,13},{10,... | collective-permute-start | bytes 786440 | tf_op jit(solution)/shard_map/ppermute | solution.py:18
  8.8 11.3 %collective-permute-start.3 = (bf16[1024,128]{1,0:T(8,128)(2,1)S(1)}, bf16[1024,128]{1,0:T(8,128)(2,1)S(1)}, u32[]{:S(2)}, u32[]{:S(2)}) collective-permute-start(bf16[1024,128]{1,0:T(8,128)(2,1)S(1)} %first_act.1.after.h0), channel_id=1, source_target_pairs={{0,6},{1,7},{2,0},{3,1},{4,2},{5,3},{6,4},{7,5},{8,14},{9,15},{10,... | collective-permute-start | bytes 786440 | tf_op jit(solution)/shard_map/ppermute | solution.py:18
  20.1 7.1 %collective-permute-start.5 = (bf16[9,2,128,128]{3,2,1,0:T(8,128)(2,1)S(1)}, bf16[9,2,128,128]{3,2,1,0:T(8,128)(2,1)S(1)}, u32[]{:S(2)}, u32[]{:S(2)}) collective-permute-start(bf16[9,2,128,128]{3,2,1,0:T(8,128)(2,1)S(1)} %collective-permute-done.got_a), channel_id=1, source_target_pairs={{0,8},{8,0},{16,24},{24,16},{32,40},{40,32},{48,56},{56,48},{64,72... | collective-permute-start | bytes 1769480 | tf_op jit(solution)/shard_map/ppermute | solution.py:22
  20.1 12.6 %collective-permute-start.4 = (bf16[3,2,128,128]{3,2,1,0:T(8,128)(2,1)S(1)}, bf16[3,2,128,128]{3,2,1,0:T(8,128)(2,1)S(1)}, u32[]{:S(2)}, u32[]{:S(2)}) collective-permute-start(bf16[3,2,128,128]{3,2,1,0:T(8,128)(2,1)S(1)} %temporal_give.1), channel_id=1, source_target_pairs={{0,129},{1,128},{2,131},{3,130},{4,133},{5,132},{6,135},{7,134},{8... | collective-permute-start | bytes 589832 | tf_op jit(solution)/shard_map/ppermute | solution.py:372
  22.8 10.2 %collective-permute-start.7 = (bf16[1024,128]{1,0:T(8,128)(2,1)S(1)}, bf16[1024,128]{1,0:T(8,128)(2,1)S(1)}, u32[]{:S(2)}, u32[]{:S(2)}) collective-permute-start(bf16[1024,128]{1,0:T(8,128)(2,1)S(1)} %bitcast.33), channel_id=1, source_target_pairs={{0,2},{1,3},{2,4},{3,5},{4,6},{5,7},{6,0},{7,1},{8,10},{9,11},{10,... | collective-permute-start | bytes 786440 | tf_op jit(solution)/shard_map/ppermute | solution.py:18
  24.1 10.7 %collective-permute-start.8 = (bf16[1024,128]{1,0:T(8,128)(2,1)S(1)}, bf16[1024,128]{1,0:T(8,128)(2,1)S(1)}, u32[]{:S(2)}, u32[]{:S(2)}) collective-permute-start(bf16[1024,128]{1,0:T(8,128)(2,1)S(1)} %bitcast.34), channel_id=1, source_target_pairs={{0,4},{1,5},{2,6},{3,7},{4,0},{5,1},{6,2},{7,3},{8,12},{9,13},{10,... | collective-permute-start | bytes 786440 | tf_op jit(solution)/shard_map/ppermute | solution.py:18
  25.7 13.4 %collective-permute-start.9 = (bf16[1024,128]{1,0:T(8,128)(2,1)S(1)}, bf16[1024,128]{1,0:T(8,128)(2,1)S(1)}, u32[]{:S(2)}, u32[]{:S(2)}) collective-permute-start(bf16[1024,128]{1,0:T(8,128)(2,1)S(1)} %bitcast.35), channel_id=1, source_target_pairs={{0,6},{1,7},{2,0},{3,1},{4,2},{5,3},{6,4},{7,5},{8,14},{9,15},{10,... | collective-permute-start | bytes 786440 | tf_op jit(solution)/shard_map/ppermute | solution.py:18
  32.6 9.8 %copy-start.1 = (bf16[3,3,1024,128]{3,2,1,0:T(8,128)(2,1)S(1)}, bf16[3,3,1024,128]{3,2,1,0:T(8,128)(2,1)}, u32[]{:S(2)}) copy-start(bf16[3,3,1024,128]{3,2,1,0:T(8,128)(2,1)} %param.6) | copy-start | bytes 7077892
  32.6 6.5 %collective-permute-start.10 = (bf16[3,2,128,128]{3,2,1,0:T(8,128)(2,1)S(1)}, bf16[3,2,128,128]{3,2,1,0:T(8,128)(2,1)S(1)}, u32[]{:S(2)}, u32[]{:S(2)}) collective-permute-start(bf16[3,2,128,128]{3,2,1,0:T(8,128)(2,1)S(1)} %collective-permute-done.4.got_a), channel_id=1, source_target_pairs={{0,8},{8,0},{16,24},{24,16},{32,40},{40,32},{48,56},{56,48},{64,72... | collective-permute-start | bytes 589832 | tf_op jit(solution)/shard_map/ppermute | solution.py:22
  32.7 15.1 %collective-permute-start.6 = (bf16[1024,128]{1,0:T(8,128)(2,1)S(1)}, bf16[1024,128]{1,0:T(8,128)(2,1)S(1)}, u32[]{:S(2)}, u32[]{:S(2)}) collective-permute-start(bf16[1024,128]{1,0:T(8,128)(2,1)S(1)} %spatial_partner.1.after), channel_id=1, source_target_pairs={{0,1},{1,0},{2,3},{3,2},{4,5},{5,4},{6,7},{7,6},{8,9},{9,8},{10,11... | collective-permute-start | bytes 786440 | tf_op jit(solution)/shard_map/ppermute | solution.py:18
  42.0 9.8 %collective-permute-start.11 = (bf16[1024,128]{1,0:T(8,128)(2,1)S(1)}, bf16[1024,128]{1,0:T(8,128)(2,1)S(1)}, u32[]{:S(2)}, u32[]{:S(2)}) collective-permute-start(bf16[1024,128]{1,0:T(8,128)(2,1)S(1)} %get-tuple-element.40), channel_id=1, source_target_pairs={{0,1},{1,0},{2,3},{3,2},{4,5},{5,4},{6,7},{7,6},{8,9},{9,8},{10,11... | collective-permute-start | bytes 786440 | tf_op jit(solution)/shard_map/ppermute | solution.py:18
  53.2 14.3 %collective-permute-start.12 = (bf16[2,1024,128]{2,1,0:T(8,128)(2,1)S(1)}, bf16[2,1024,128]{2,1,0:T(8,128)(2,1)S(1)}, u32[]{:S(2)}, u32[]{:S(2)}) collective-permute-start(bf16[2,1024,128]{2,1,0:T(8,128)(2,1)S(1)} %second_act.1.b0), channel_id=1, source_target_pairs={{0,1},{1,0},{2,3},{3,2},{4,5},{5,4},{6,7},{7,6},{8,9},{9,8},{10,11... | collective-permute-start | bytes 1572872 | tf_op jit(solution)/shard_map/ppermute | solution.py:18
  54.5 1.4 copy-start.2
  72.1 6.5 %collective-permute-start.13 = (bf16[2,8,6,32,128]{4,3,2,1,0:T(8,128)(2,1)S(1)}, bf16[2,8,6,32,128]{4,3,2,1,0:T(8,128)(2,1)S(1)}, u32[]{:S(2)}, u32[]{:S(2)}) collective-permute-start(bf16[2,8,6,32,128]{4,3,2,1,0:T(8,128)(2,1)S(1)} %get-tuple-element.41.after), channel_id=1, source_target_pairs={{0,8},{8,0},{16,24},{24,16},{32,40},{40,32},{48,56},{56,48},{64,72... | collective-permute-start | bytes 2359304 | tf_op jit(solution)/shard_map/ppermute | solution.py:22
  78.1 2.4 %collective-permute-start.15 = (bf16[2,8,6,32,128]{4,3,2,1,0:T(8,128)(2,1)S(1)}, bf16[2,8,6,32,128]{4,3,2,1,0:T(8,128)(2,1)S(1)}, u32[]{:S(2)}, u32[]{:S(2)}) collective-permute-start(bf16[2,8,6,32,128]{4,3,2,1,0:T(8,128)(2,1)S(1)} %get-tuple-element.42.after), channel_id=1, source_target_pairs={{0,8},{8,0},{16,24},{24,16},{32,40},{40,32},{48,56},{56,48},{64,72... | collective-permute-start | bytes 2359304 | tf_op jit(solution)/shard_map/ppermute | solution.py:22
  79.0 1.7 %copy-start.7 = (f32[2,8,6,32,128]{4,3,2,1,0:T(8,128)S(1)}, f32[2,8,6,32,128]{4,3,2,1,0:T(8,128)}, u32[]{:S(2)}) copy-start(f32[2,8,6,32,128]{4,3,2,1,0:T(8,128)} %get-tuple-element.46) | copy-start | bytes 4718596
  79.0 12.1 %collective-permute-start.14 = (bf16[8,6,32,128]{3,2,1,0:T(8,128)(2,1)S(1)}, bf16[8,6,32,128]{3,2,1,0:T(8,128)(2,1)S(1)}, u32[]{:S(2)}, u32[]{:S(2)}) collective-permute-start(bf16[8,6,32,128]{3,2,1,0:T(8,128)(2,1)S(1)} %fusion.8), channel_id=1, source_target_pairs={{0,128},{8,136},{16,144},{24,152},{32,160},{40,168},{48,176},{56,1... | collective-permute-start | bytes 1179656 | tf_op jit(solution)/shard_map/ppermute | solution.py:22
  80.9 17.6 %collective-permute-start.16 = (bf16[8,6,32,128]{3,2,1,0:T(8,128)(2,1)S(1)}, bf16[8,6,32,128]{3,2,1,0:T(8,128)(2,1)S(1)}, u32[]{:S(2)}, u32[]{:S(2)}) collective-permute-start(bf16[8,6,32,128]{3,2,1,0:T(8,128)(2,1)S(1)} %fusion.9), channel_id=1, source_target_pairs={{0,128},{8,136},{16,144},{24,152},{32,160},{40,168},{48,176},{56,1... | collective-permute-start | bytes 1179656 | tf_op jit(solution)/shard_map/ppermute | solution.py:22
  90.2 8.6 %copy-start.6 = (bf16[2,1024,128]{2,1,0:T(8,128)(2,1)}, bf16[2,1024,128]{2,1,0:T(8,128)(2,1)S(1)}, u32[]{:S(2)}) copy-start(bf16[2,1024,128]{2,1,0:T(8,128)(2,1)S(1)} %get-tuple-element.52) | copy-start | bytes 1572868
  99.8 31.1 %all-to-all-start = ((bf16[8,12,32,128]{3,2,1,0:T(8,128)(2,1)}), bf16[8,12,32,128]{3,2,1,0:T(8,128)(2,1)}, u32[]{:S(2)}, u32[]{:S(2)}) async-start(bf16[8,12,32,128]{3,2,1,0:T(8,128)(2,1)} %pad_maximum_fusion), calls=%async_computation | async-start | bytes 1572864 | tf_op jit(solution)/shard_map/all_to_all | solution.py:474
  108.3 25.8 %collective-permute-start.17 = (bf16[2,1024,128]{2,1,0:T(8,128)(2,1)}, bf16[2,1024,128]{2,1,0:T(8,128)(2,1)S(1)}, u32[]{:S(2)}, u32[]{:S(2)}) collective-permute-start(bf16[2,1024,128]{2,1,0:T(8,128)(2,1)} %get-tuple-element.50), channel_id=1, source_target_pairs={{0,2},{1,3},{2,4},{3,5},{4,6},{5,7},{6,0},{7,1},{8,10},{9,11},{10,... | collective-permute-start | bytes 1572872 | tf_op jit(solution)/shard_map/ppermute | solution.py:18
  108.3 25.8 %collective-permute-start.18 = (bf16[2,1024,128]{2,1,0:T(8,128)(2,1)}, bf16[2,1024,128]{2,1,0:T(8,128)(2,1)S(1)}, u32[]{:S(2)}, u32[]{:S(2)}) collective-permute-start(bf16[2,1024,128]{2,1,0:T(8,128)(2,1)} %get-tuple-element.51), channel_id=1, source_target_pairs={{0,4},{1,5},{2,6},{3,7},{4,0},{5,1},{6,2},{7,3},{8,12},{9,13},{10,... | collective-permute-start | bytes 1572872 | tf_op jit(solution)/shard_map/ppermute | solution.py:18
  110.6 23.5 %collective-permute-start.19 = (bf16[2,1024,128]{2,1,0:T(8,128)(2,1)}, bf16[2,1024,128]{2,1,0:T(8,128)(2,1)S(1)}, u32[]{:S(2)}, u32[]{:S(2)}) collective-permute-start(bf16[2,1024,128]{2,1,0:T(8,128)(2,1)} %copy-done.6), channel_id=1, source_target_pairs={{0,6},{1,7},{2,0},{3,1},{4,2},{5,3},{6,4},{7,5},{8,14},{9,15},{10,... | collective-permute-start | bytes 1572872 | tf_op jit(solution)/shard_map/ppermute | solution.py:18
  132.1 11.0 %collective-permute-start.20 = (bf16[12,32,128]{2,1,0:T(8,128)(2,1)S(1)}, bf16[12,32,128]{2,1,0:T(8,128)(2,1)S(1)}, u32[]{:S(2)}, u32[]{:S(2)}) collective-permute-start(bf16[12,32,128]{2,1,0:T(8,128)(2,1)S(1)} %multiply_convert_fusion), channel_id=1, source_target_pairs={{1,32},{3,34},{5,36},{7,38},{9,40},{11,42},{13,44},{15,46},{17,48}... | collective-permute-start | bytes 294920 | tf_op jit(solution)/shard_map/ppermute | solution.py:488

commit v4 on v3

--- a/solution.py
+++ b/solution.py
@@ -201,12 +201,12 @@
         unfold(piece[...], wide, lambda sa, sb: block(((sa + 1) * 3 + sb + 1) * 4 + yb))
 
     def step(i, carry):
-        rows = pl.ds(pl.multiple_of(i * 256, 256), 256)
-        left = wide[pl.ds(2 * i, 2)].reshape(256, 4608)
+        rows = pl.ds(pl.multiple_of(i * 512, 512), 512)
+        left = wide[pl.ds(4 * i, 4)].reshape(512, 4608)
         result[rows, :] = jnp.dot(left, half[...], preferred_element_type=F32).astype(result.dtype)
         return carry
 
-    lax.fori_loop(0, 4, step, 0)
+    lax.fori_loop(0, 2, step, 0)
 
 
 def spatial_partner_kernel(place, h0, h1, h2, h3, got_a, got_b, give, half, wide):

time: 145 us -> 145 us (level)
  transfers between devices with their start and end apart: 22 -> 22, of which waited for: 12 -> 12; matrix products, arithmetic and copies ran while one was open for 2% -> 2% of each run, Pallas kernels for 23% -> 22%
where the time goes in v4:
time: 145 us; the launch traced here: 144 us
  waiting for transfers between devices  66 us (46%)
  Pallas kernels  38.8 us (27%)
  starting transfers between devices  30.7 us (21%)
  local copies, waits for them, and re-layouts  4.35 us (3%)
  other arithmetic  3.55 us (2%)
    pallas_call x12, Pallas kernels, call(): pl.pallas_call(body, out_shape=outs, in_specs=specs, out_specs=[vmem] * l...  38.8 us
    ppermute x12, waiting for transfers between devices, tensor_move(): return lax.ppermute(values, 'tensor', pairs)  32.2 us
    all_to_all x1, waiting for transfers between devices, per_device(): lax.all_to_all(local, 'dp', split_axis=0, concat_axis=0, tiled=True, axis...  17.7 us
    ppermute x12, starting transfers between devices, tensor_move(): return lax.ppermute(values, 'tensor', pairs)  15.4 us
    ppermute x6, waiting for transfers between devices, data_move(): return lax.ppermute(values, 'dp', [(d, d ^ bits) for d in range(32)])  9.54 us
    all_to_all x1, starting transfers between devices, per_device(): lax.all_to_all(local, 'dp', split_axis=0, concat_axis=0, tiled=True, axis...  8.51 us
    ppermute x1, waiting for transfers between devices, per_device(): moved = lax.ppermute(share, ('dp', 'tensor'), move)  6.46 us
    unnamed x16, local copies, waits for them, and re-layouts  3.1 us
  transfers between devices with their start and end apart: 22, of which 12 were waited for; matrix products, arithmetic and copies ran while one was open for 2% of the time, Pallas kernels for 22%

profile of v4, /device:TPU:14, one launch (start us, length us, event | category | flops | bytes accessed | tf_op | source)
XLA Modules:
  0.0 144.4 jit_solution(3370413142892520634)
XLA Ops:
  0.7 1.7 %copy-done = bf16[3,3,1024,128]{3,2,1,0:T(8,128)(2,1)S(1)} copy-done((bf16[3,3,1024,128]{3,2,1,0:T(8,128)(2,1)S(1)}, bf16[3,3,1024,128]{3,2,1,0:T(8,128)(2,1)}, u32[]{:S(2)}) %copy-start) | copy-done | bytes 2359320
  2.4 0.6 spatial_give.1.after
  3.0 0.6 collective-permute-start
  3.6 0.8 first_act.1.after.h0
  4.4 1.7 %collective-permute-start.1 = (bf16[1024,128]{1,0:T(8,128)(2,1)S(1)}, bf16[1024,128]{1,0:T(8,128)(2,1)S(1)}, u32[]{:S(2)}, u32[]{:S(2)}) collective-permute-start(bf16[1024,128]{1,0:T(8,128)(2,1)S(1)} %first_act.1.after.h0), channel_id=1, source_target_pairs={{0,2},{1,3},{2,4},{3,5},{4,6},{5,7},{6,0},{7,1},{8,10},{9,11},{10,... | collective-permute-start | bytes 786440 | tf_op jit(solution)/shard_map/ppermute | solution.py:18
  6.1 2.7 %collective-permute-start.2 = (bf16[1024,128]{1,0:T(8,128)(2,1)S(1)}, bf16[1024,128]{1,0:T(8,128)(2,1)S(1)}, u32[]{:S(2)}, u32[]{:S(2)}) collective-permute-start(bf16[1024,128]{1,0:T(8,128)(2,1)S(1)} %first_act.1.after.h0), channel_id=1, source_target_pairs={{0,4},{1,5},{2,6},{3,7},{4,0},{5,1},{6,2},{7,3},{8,12},{9,13},{10,... | collective-permute-start | bytes 786440 | tf_op jit(solution)/shard_map/ppermute | solution.py:18
  8.8 0.7 collective-permute-start.3
  9.5 0.6 temporal_give.1
  10.1 3.9 %collective-permute-done.1.h1 = bf16[1024,128]{1,0:T(8,128)(2,1)S(1)} collective-permute-done((bf16[1024,128]{1,0:T(8,128)(2,1)S(1)}, bf16[1024,128]{1,0:T(8,128)(2,1)S(1)}, u32[]{:S(2)}, u32[]{:S(2)}) %collective-permute-start.1) | collective-permute-done | bytes 262176 | tf_op jit(solution)/shard_map/ppermute | solution.py:18
  13.9 2.9 %collective-permute-done.2.h2 = bf16[1024,128]{1,0:T(8,128)(2,1)S(1)} collective-permute-done((bf16[1024,128]{1,0:T(8,128)(2,1)S(1)}, bf16[1024,128]{1,0:T(8,128)(2,1)S(1)}, u32[]{:S(2)}, u32[]{:S(2)}) %collective-permute-start.2) | collective-permute-done | bytes 262176 | tf_op jit(solution)/shard_map/ppermute | solution.py:18
  16.9 3.2 %collective-permute-done.3.h3 = bf16[1024,128]{1,0:T(8,128)(2,1)S(1)} collective-permute-done((bf16[1024,128]{1,0:T(8,128)(2,1)S(1)}, bf16[1024,128]{1,0:T(8,128)(2,1)S(1)}, u32[]{:S(2)}, u32[]{:S(2)}) %collective-permute-start.3) | collective-permute-done | bytes 262176 | tf_op jit(solution)/shard_map/ppermute | solution.py:18
  20.1 2.7 %collective-permute-start.4 = (bf16[3,2,128,128]{3,2,1,0:T(8,128)(2,1)S(1)}, bf16[3,2,128,128]{3,2,1,0:T(8,128)(2,1)S(1)}, u32[]{:S(2)}, u32[]{:S(2)}) collective-permute-start(bf16[3,2,128,128]{3,2,1,0:T(8,128)(2,1)S(1)} %temporal_give.1), channel_id=1, source_target_pairs={{0,129},{1,128},{2,131},{3,130},{4,133},{5,132},{6,135},{7,134},{8... | collective-permute-start | bytes 589832 | tf_op jit(solution)/shard_map/ppermute | solution.py:372
  22.8 1.3 collective-permute-start.7
  24.1 1.7 %collective-permute-start.8 = (bf16[1024,128]{1,0:T(8,128)(2,1)S(1)}, bf16[1024,128]{1,0:T(8,128)(2,1)S(1)}, u32[]{:S(2)}, u32[]{:S(2)}) collective-permute-start(bf16[1024,128]{1,0:T(8,128)(2,1)S(1)} %bitcast.34), channel_id=1, source_target_pairs={{0,4},{1,5},{2,6},{3,7},{4,0},{5,1},{6,2},{7,3},{8,12},{9,13},{10,... | collective-permute-start | bytes 786440 | tf_op jit(solution)/shard_map/ppermute | solution.py:18
  25.7 1.5 %collective-permute-start.9 = (bf16[1024,128]{1,0:T(8,128)(2,1)S(1)}, bf16[1024,128]{1,0:T(8,128)(2,1)S(1)}, u32[]{:S(2)}, u32[]{:S(2)}) collective-permute-start(bf16[1024,128]{1,0:T(8,128)(2,1)S(1)} %bitcast.35), channel_id=1, source_target_pairs={{0,6},{1,7},{2,0},{3,1},{4,2},{5,3},{6,4},{7,5},{8,14},{9,15},{10,... | collective-permute-start | bytes 786440 | tf_op jit(solution)/shard_map/ppermute | solution.py:18
  27.2 5.1 %spatial_partner.1.after = bf16[1024,128]{1,0:T(8,128)(2,1)S(1)} custom-call(s32[4]{0:T(128)S(1)} %pad_add_fusion.place, bf16[1024,128]{1,0:T(8,128)(2,1)S(1)} %first_act.1.after.h0, bf16[1024,128]{1,0:T(8,128)(2,1)S(1)} %collective-permute-done.1.h1, bf16[1024,128]{1,0:T(8,128)(2,1)S(1)} %collective-permute-done.2.h2, ...), custom_call_target="tpu_custom_call" | custom-call | flops 1207959552 | bytes 2490384 | tf_op jit(solution)/shard_map/spatial_partner/pallas_call | solution.py:37
  32.4 0.3 collective-permute-start.6
  32.7 2.0 %collective-permute-done.8.g2 = bf16[1024,128]{1,0:T(8,128)(2,1)S(1)} collective-permute-done((bf16[1024,128]{1,0:T(8,128)(2,1)S(1)}, bf16[1024,128]{1,0:T(8,128)(2,1)S(1)}, u32[]{:S(2)}, u32[]{:S(2)}) %collective-permute-start.8) | collective-permute-done | bytes 262176 | tf_op jit(solution)/shard_map/ppermute | solution.py:18
  34.8 4.4 %collective-permute-done.9.g3 = bf16[1024,128]{1,0:T(8,128)(2,1)S(1)} collective-permute-done((bf16[1024,128]{1,0:T(8,128)(2,1)S(1)}, bf16[1024,128]{1,0:T(8,128)(2,1)S(1)}, u32[]{:S(2)}, u32[]{:S(2)}) %collective-permute-start.9) | collective-permute-done | bytes 262176 | tf_op jit(solution)/shard_map/ppermute | solution.py:18
  39.2 2.8 %grad_second.1 = (f32[1024,128]{1,0:T(8,128)S(1)}, bf16[1024,128]{1,0:T(8,128)(2,1)S(1)}) custom-call(s32[4]{0:T(128)S(1)} %pad_add_fusion.place, bf16[1024,128]{1,0:T(8,128)(2,1)S(1)} %bitcast.36, bf16[1024,128]{1,0:T(8,128)(2,1)S(1)} %collective-permute-done.7.g1, bf16[1024,128]{1,0:T(8,128)(2,1)S(1)} %collective-permute-done.8.g2, ...), custom_call_target="tpu_custom_call" | custom-call | flops 805306368 | bytes 3276816 | tf_op jit(solution)/shard_map/grad_second/pallas_call | solution.py:37
  42.0 0.4 collective-permute-start.11
  42.4 5.1 %spatial_own.1.out_own = f32[1024,128]{1,0:T(8,128)S(1)} custom-call(s32[4]{0:T(128)S(1)} %pad_add_fusion.place, bf16[1024,128]{1,0:T(8,128)(2,1)S(1)} %first_act.1.after.h0, bf16[1024,128]{1,0:T(8,128)(2,1)S(1)} %collective-permute-done.1.h1, bf16[1024,128]{1,0:T(8,128)(2,1)S(1)} %collective-permute-done.2.h2, ...), custom_call_target="tpu_custom_call" | custom-call | flops 1207959552 | bytes 4194320 | tf_op jit(solution)/shard_map/spatial_own/pallas_call | solution.py:37
  47.5 4.2 %collective-permute-done.11.grad_got = bf16[1024,128]{1,0:T(8,128)(2,1)S(1)} collective-permute-done((bf16[1024,128]{1,0:T(8,128)(2,1)S(1)}, bf16[1024,128]{1,0:T(8,128)(2,1)S(1)}, u32[]{:S(2)}, u32[]{:S(2)}) %collective-permute-start.11) | collective-permute-done | bytes 262176 | tf_op jit(solution)/shard_map/ppermute | solution.py:18
  51.8 1.4 second_act.1.b0
  53.2 0.4 collective-permute-start.12
  53.6 1.0 spatial_pair.1.after.spatial
  54.6 1.4 copy-done.2
  56.0 11.6 %collective-permute-done.12.b1 = bf16[2,1024,128]{2,1,0:T(8,128)(2,1)S(1)} collective-permute-done((bf16[2,1024,128]{2,1,0:T(8,128)(2,1)S(1)}, bf16[2,1024,128]{2,1,0:T(8,128)(2,1)S(1)}, u32[]{:S(2)}, u32[]{:S(2)}) %collective-permute-start.12) | collective-permute-done | bytes 524320 | tf_op jit(solution)/shard_map/ppermute | solution.py:18
  67.5 4.5 %early_grads.1 = (f32[2,8,6,32,128]{4,3,2,1,0:T(8,128)S(1)}, bf16[2,8,6,32,128]{4,3,2,1,0:T(8,128)(2,1)S(1)}) custom-call(s32[4]{0:T(128)S(1)} %pad_add_fusion.place, bf16[1024,128]{1,0:T(8,128)(2,1)S(1)} %first_act.1.after.h0, bf16[1024,128]{1,0:T(8,128)(2,1)S(1)} %collective-permute-done.1.h1, bf16[1024,128]{1,0:T(8,128)(2,1)S(1)} %collective-permute-done.2.h2, ...), custom_call_target="tpu_custom_call" | custom-call | flops 1610612736 | bytes 6815760 | tf_op jit(solution)/shard_map/early_grads/pallas_call | solution.py:37
  72.2 5.9 %late_grads.1 = (f32[2,8,6,32,128]{4,3,2,1,0:T(8,128)}, bf16[2,8,6,32,128]{4,3,2,1,0:T(8,128)(2,1)S(1)}) custom-call(s32[4]{0:T(128)S(1)} %pad_add_fusion.place, bf16[1024,128]{1,0:T(8,128)(2,1)S(1)} %first_act.1.after.h0, bf16[1024,128]{1,0:T(8,128)(2,1)S(1)} %collective-permute-done.1.h1, bf16[1024,128]{1,0:T(8,128)(2,1)S(1)} %collective-permute-done.2.h2, ...), custom_call_target="tpu_custom_call" | custom-call | flops 1610612736 | bytes 6291472 | tf_op jit(solution)/shard_map/late_grads/pallas_call | solution.py:37
  78.1 0.5 collective-permute-start.15
  79.1 1.4 collective-permute-done.15
  80.9 0.9 collective-permute-start.16
  81.8 8.4 %both_back.1 = (f32[1024,128]{1,0:T(8,128)S(1)}, f32[1024,128]{1,0:T(8,128)S(1)}, bf16[2,1024,128]{2,1,0:T(8,128)(2,1)}, bf16[2,1024,128]{2,1,0:T(8,128)(2,1)}, bf16[2,1024,128]{2,1,0:T(8,128)(2,1)S(1)}) custom-call(s32[4]{0:T(128)S(1)} %pad_add_fusion.place, bf16[2,1024,128]{2,1,0:T(8,128)(2,1)S(1)} %second_act.1.b0, ...), custom_call_target="tpu_custom_call" | custom-call | flops 3221225472 | bytes 7995408 | tf_op jit(solution)/shard_map/both_back/pallas_call | solution.py:37
  90.2 0.8 collective-permute-done.14
  91.3 7.3 %collective-permute-done.16 = bf16[8,6,32,128]{3,2,1,0:T(8,128)(2,1)S(1)} collective-permute-done((bf16[8,6,32,128]{3,2,1,0:T(8,128)(2,1)S(1)}, bf16[8,6,32,128]{3,2,1,0:T(8,128)(2,1)S(1)}, u32[]{:S(2)}, u32[]{:S(2)}) %collective-permute-start.16) | collective-permute-done | bytes 393248 | tf_op jit(solution)/shard_map/ppermute | solution.py:22
  98.5 0.2 fusion.3
  98.8 1.0 pad_maximum_fusion
  99.8 8.5 %all-to-all-start = ((bf16[8,12,32,128]{3,2,1,0:T(8,128)(2,1)}), bf16[8,12,32,128]{3,2,1,0:T(8,128)(2,1)}, u32[]{:S(2)}, u32[]{:S(2)}) async-start(bf16[8,12,32,128]{3,2,1,0:T(8,128)(2,1)} %pad_maximum_fusion), calls=%async_computation | async-start | bytes 1572864 | tf_op jit(solution)/shard_map/all_to_all | solution.py:474
  108.3 2.3 %collective-permute-start.18 = (bf16[2,1024,128]{2,1,0:T(8,128)(2,1)}, bf16[2,1024,128]{2,1,0:T(8,128)(2,1)S(1)}, u32[]{:S(2)}, u32[]{:S(2)}) collective-permute-start(bf16[2,1024,128]{2,1,0:T(8,128)(2,1)} %get-tuple-element.51), channel_id=1, source_target_pairs={{0,4},{1,5},{2,6},{3,7},{4,0},{5,1},{6,2},{7,3},{8,12},{9,13},{10,... | collective-permute-start | bytes 1572872 | tf_op jit(solution)/shard_map/ppermute | solution.py:18
  110.6 2.5 %collective-permute-start.19 = (bf16[2,1024,128]{2,1,0:T(8,128)(2,1)}, bf16[2,1024,128]{2,1,0:T(8,128)(2,1)S(1)}, u32[]{:S(2)}, u32[]{:S(2)}) collective-permute-start(bf16[2,1024,128]{2,1,0:T(8,128)(2,1)} %copy-done.6), channel_id=1, source_target_pairs={{0,6},{1,7},{2,0},{3,1},{4,2},{5,3},{6,4},{7,5},{8,14},{9,15},{10,... | collective-permute-start | bytes 1572872 | tf_op jit(solution)/shard_map/ppermute | solution.py:18
  113.1 17.7 %all-to-all-done = bf16[8,12,32,128]{3,2,1,0:T(8,128)(2,1)} async-done(((bf16[8,12,32,128]{3,2,1,0:T(8,128)(2,1)}), bf16[8,12,32,128]{3,2,1,0:T(8,128)(2,1)}, u32[]{:S(2)}, u32[]{:S(2)}) %all-to-all-start) | async-done | bytes 786464 | tf_op jit(solution)/shard_map/all_to_all | solution.py:474
  130.8 1.3 convert_reduce_fusion
  132.1 1.9 %collective-permute-start.20 = (bf16[12,32,128]{2,1,0:T(8,128)(2,1)S(1)}, bf16[12,32,128]{2,1,0:T(8,128)(2,1)S(1)}, u32[]{:S(2)}, u32[]{:S(2)}) collective-permute-start(bf16[12,32,128]{2,1,0:T(8,128)(2,1)S(1)} %multiply_convert_fusion), channel_id=1, source_target_pairs={{1,32},{3,34},{5,36},{7,38},{9,40},{11,42},{13,44},{15,46},{17,48}... | collective-permute-start | bytes 294920 | tf_op jit(solution)/shard_map/ppermute | solution.py:488
  134.1 2.5 %finish.1 = (bf16[1024,128]{1,0:T(8,128)(2,1)}, bf16[1024,128]{1,0:T(8,128)(2,1)}) custom-call(bf16[1024,128]{1,0:T(8,128)(2,1)S(1)} %bitcast.32, bf16[1024,128]{1,0:T(8,128)(2,1)S(1)} %bitcast.38, f32[1024,128]{1,0:T(8,128)S(1)} %get-tuple-element.43.own_back, f32[1024,128]{1,0:T(8,128)S(1)} %get-tuple-element.44.own_ahead, ...), custom_call_target="tpu_custom_call" | custom-call | flops 10000000 | bytes 3670016 | tf_op jit(solution)/shard_map/finish/pallas_call | solution.py:37
  136.6 6.5 %collective-permute-done.20 = bf16[12,32,128]{2,1,0:T(8,128)(2,1)S(1)} collective-permute-done((bf16[12,32,128]{2,1,0:T(8,128)(2,1)S(1)}, bf16[12,32,128]{2,1,0:T(8,128)(2,1)S(1)}, u32[]{:S(2)}, u32[]{:S(2)}) %collective-permute-start.20) | collective-permute-done | bytes 98336 | tf_op jit(solution)/shard_map/ppermute | solution.py:488
  143.1 0.6 slice.44
  143.8 0.6 slice_bitcast_fusion
  (37 shorter events, 1.4 us)
Async XLA Ops:
  0.7 1.7 %copy-start = (bf16[3,3,1024,128]{3,2,1,0:T(8,128)(2,1)S(1)}, bf16[3,3,1024,128]{3,2,1,0:T(8,128)(2,1)}, u32[]{:S(2)}) copy-start(bf16[3,3,1024,128]{3,2,1,0:T(8,128)(2,1)} %param.6) | copy-start | bytes 7077892
  2.4 1.2 copy-start.3
  2.4 7.0 %copy-start.4 = (bf16[3,128,1024]{2,1,0:T(8,128)(2,1)S(1)}, bf16[3,128,1024]{2,1,0:T(8,128)(2,1)}, u32[]{:S(2)}) copy-start(bf16[3,128,1024]{2,1,0:T(8,128)(2,1)} %temporal.1) | copy-start | bytes 2359300
  3.0 19.8 %copy-start.5 = (bf16[1,8,8,16,128]{4,3,2,1,0:T(8,128)(2,1)S(1)}, bf16[1,8,8,16,128]{4,3,2,1,0:T(8,128)(2,1)}, u32[]{:S(2)}) copy-start(bf16[1,8,8,16,128]{4,3,2,1,0:T(8,128)(2,1)} %param.5) | copy-start | bytes 786436
  3.0 17.1 %collective-permute-start = (bf16[9,2,128,128]{3,2,1,0:T(8,128)(2,1)S(1)}, bf16[9,2,128,128]{3,2,1,0:T(8,128)(2,1)S(1)}, u32[]{:S(2)}, u32[]{:S(2)}) collective-permute-start(bf16[9,2,128,128]{3,2,1,0:T(8,128)(2,1)S(1)} %spatial_give.1.after), channel_id=1, source_target_pairs={{0,129},{1,128},{2,131},{3,130},{4,133},{5,132},{6,135},{7,134},{8... | collective-permute-start | bytes 1769480 | tf_op jit(solution)/shard_map/ppermute | solution.py:356
  4.4 9.5 %collective-permute-start.1 = (bf16[1024,128]{1,0:T(8,128)(2,1)S(1)}, bf16[1024,128]{1,0:T(8,128)(2,1)S(1)}, u32[]{:S(2)}, u32[]{:S(2)}) collective-permute-start(bf16[1024,128]{1,0:T(8,128)(2,1)S(1)} %first_act.1.after.h0), channel_id=1, source_target_pairs={{0,2},{1,3},{2,4},{3,5},{4,6},{5,7},{6,0},{7,1},{8,10},{9,11},{10,... | collective-permute-start | bytes 786440 | tf_op jit(solution)/shard_map/ppermute | solution.py:18
  6.1 10.8 %collective-permute-start.2 = (bf16[1024,128]{1,0:T(8,128)(2,1)S(1)}, bf16[1024,128]{1,0:T(8,128)(2,1)S(1)}, u32[]{:S(2)}, u32[]{:S(2)}) collective-permute-start(bf16[1024,128]{1,0:T(8,128)(2,1)S(1)} %first_act.1.after.h0), channel_id=1, source_target_pairs={{0,4},{1,5},{2,6},{3,7},{4,0},{5,1},{6,2},{7,3},{8,12},{9,13},{10,... | collective-permute-start | bytes 786440 | tf_op jit(solution)/shard_map/ppermute | solution.py:18
  8.8 11.3 %collective-permute-start.3 = (bf16[1024,128]{1,0:T(8,128)(2,1)S(1)}, bf16[1024,128]{1,0:T(8,128)(2,1)S(1)}, u32[]{:S(2)}, u32[]{:S(2)}) collective-permute-start(bf16[1024,128]{1,0:T(8,128)(2,1)S(1)} %first_act.1.after.h0), channel_id=1, source_target_pairs={{0,6},{1,7},{2,0},{3,1},{4,2},{5,3},{6,4},{7,5},{8,14},{9,15},{10,... | collective-permute-start | bytes 786440 | tf_op jit(solution)/shard_map/ppermute | solution.py:18
  20.1 7.1 %collective-permute-start.5 = (bf16[9,2,128,128]{3,2,1,0:T(8,128)(2,1)S(1)}, bf16[9,2,128,128]{3,2,1,0:T(8,128)(2,1)S(1)}, u32[]{:S(2)}, u32[]{:S(2)}) collective-permute-start(bf16[9,2,128,128]{3,2,1,0:T(8,128)(2,1)S(1)} %collective-permute-done.got_a), channel_id=1, source_target_pairs={{0,8},{8,0},{16,24},{24,16},{32,40},{40,32},{48,56},{56,48},{64,72... | collective-permute-start | bytes 1769480 | tf_op jit(solution)/shard_map/ppermute | solution.py:22
  20.1 12.3 %collective-permute-start.4 = (bf16[3,2,128,128]{3,2,1,0:T(8,128)(2,1)S(1)}, bf16[3,2,128,128]{3,2,1,0:T(8,128)(2,1)S(1)}, u32[]{:S(2)}, u32[]{:S(2)}) collective-permute-start(bf16[3,2,128,128]{3,2,1,0:T(8,128)(2,1)S(1)} %temporal_give.1), channel_id=1, source_target_pairs={{0,129},{1,128},{2,131},{3,130},{4,133},{5,132},{6,135},{7,134},{8... | collective-permute-start | bytes 589832 | tf_op jit(solution)/shard_map/ppermute | solution.py:372
  22.8 9.9 %collective-permute-start.7 = (bf16[1024,128]{1,0:T(8,128)(2,1)S(1)}, bf16[1024,128]{1,0:T(8,128)(2,1)S(1)}, u32[]{:S(2)}, u32[]{:S(2)}) collective-permute-start(bf16[1024,128]{1,0:T(8,128)(2,1)S(1)} %bitcast.33), channel_id=1, source_target_pairs={{0,2},{1,3},{2,4},{3,5},{4,6},{5,7},{6,0},{7,1},{8,10},{9,11},{10,... | collective-permute-start | bytes 786440 | tf_op jit(solution)/shard_map/ppermute | solution.py:18
  24.1 10.7 %collective-permute-start.8 = (bf16[1024,128]{1,0:T(8,128)(2,1)S(1)}, bf16[1024,128]{1,0:T(8,128)(2,1)S(1)}, u32[]{:S(2)}, u32[]{:S(2)}) collective-permute-start(bf16[1024,128]{1,0:T(8,128)(2,1)S(1)} %bitcast.34), channel_id=1, source_target_pairs={{0,4},{1,5},{2,6},{3,7},{4,0},{5,1},{6,2},{7,3},{8,12},{9,13},{10,... | collective-permute-start | bytes 786440 | tf_op jit(solution)/shard_map/ppermute | solution.py:18
  25.7 13.4 %collective-permute-start.9 = (bf16[1024,128]{1,0:T(8,128)(2,1)S(1)}, bf16[1024,128]{1,0:T(8,128)(2,1)S(1)}, u32[]{:S(2)}, u32[]{:S(2)}) collective-permute-start(bf16[1024,128]{1,0:T(8,128)(2,1)S(1)} %bitcast.35), channel_id=1, source_target_pairs={{0,6},{1,7},{2,0},{3,1},{4,2},{5,3},{6,4},{7,5},{8,14},{9,15},{10,... | collective-permute-start | bytes 786440 | tf_op jit(solution)/shard_map/ppermute | solution.py:18
  32.3 10.1 %copy-start.1 = (bf16[3,3,1024,128]{3,2,1,0:T(8,128)(2,1)S(1)}, bf16[3,3,1024,128]{3,2,1,0:T(8,128)(2,1)}, u32[]{:S(2)}) copy-start(bf16[3,3,1024,128]{3,2,1,0:T(8,128)(2,1)} %param.6) | copy-start | bytes 7077892
  32.3 6.8 %collective-permute-start.10 = (bf16[3,2,128,128]{3,2,1,0:T(8,128)(2,1)S(1)}, bf16[3,2,128,128]{3,2,1,0:T(8,128)(2,1)S(1)}, u32[]{:S(2)}, u32[]{:S(2)}) collective-permute-start(bf16[3,2,128,128]{3,2,1,0:T(8,128)(2,1)S(1)} %collective-permute-done.4.got_a), channel_id=1, source_target_pairs={{0,8},{8,0},{16,24},{24,16},{32,40},{40,32},{48,56},{56,48},{64,72... | collective-permute-start | bytes 589832 | tf_op jit(solution)/shard_map/ppermute | solution.py:22
  32.4 15.1 %collective-permute-start.6 = (bf16[1024,128]{1,0:T(8,128)(2,1)S(1)}, bf16[1024,128]{1,0:T(8,128)(2,1)S(1)}, u32[]{:S(2)}, u32[]{:S(2)}) collective-permute-start(bf16[1024,128]{1,0:T(8,128)(2,1)S(1)} %spatial_partner.1.after), channel_id=1, source_target_pairs={{0,1},{1,0},{2,3},{3,2},{4,5},{5,4},{6,7},{7,6},{8,9},{9,8},{10,11... | collective-permute-start | bytes 786440 | tf_op jit(solution)/shard_map/ppermute | solution.py:18
  42.0 9.8 %collective-permute-start.11 = (bf16[1024,128]{1,0:T(8,128)(2,1)S(1)}, bf16[1024,128]{1,0:T(8,128)(2,1)S(1)}, u32[]{:S(2)}, u32[]{:S(2)}) collective-permute-start(bf16[1024,128]{1,0:T(8,128)(2,1)S(1)} %get-tuple-element.40), channel_id=1, source_target_pairs={{0,1},{1,0},{2,3},{3,2},{4,5},{5,4},{6,7},{7,6},{8,9},{9,8},{10,11... | collective-permute-start | bytes 786440 | tf_op jit(solution)/shard_map/ppermute | solution.py:18
  53.2 14.3 %collective-permute-start.12 = (bf16[2,1024,128]{2,1,0:T(8,128)(2,1)S(1)}, bf16[2,1024,128]{2,1,0:T(8,128)(2,1)S(1)}, u32[]{:S(2)}, u32[]{:S(2)}) collective-permute-start(bf16[2,1024,128]{2,1,0:T(8,128)(2,1)S(1)} %second_act.1.b0), channel_id=1, source_target_pairs={{0,1},{1,0},{2,3},{3,2},{4,5},{5,4},{6,7},{7,6},{8,9},{9,8},{10,11... | collective-permute-start | bytes 1572872 | tf_op jit(solution)/shard_map/ppermute | solution.py:18
  54.5 1.4 copy-start.2
  72.1 6.5 %collective-permute-start.13 = (bf16[2,8,6,32,128]{4,3,2,1,0:T(8,128)(2,1)S(1)}, bf16[2,8,6,32,128]{4,3,2,1,0:T(8,128)(2,1)S(1)}, u32[]{:S(2)}, u32[]{:S(2)}) collective-permute-start(bf16[2,8,6,32,128]{4,3,2,1,0:T(8,128)(2,1)S(1)} %get-tuple-element.41.after), channel_id=1, source_target_pairs={{0,8},{8,0},{16,24},{24,16},{32,40},{40,32},{48,56},{56,48},{64,72... | collective-permute-start | bytes 2359304 | tf_op jit(solution)/shard_map/ppermute | solution.py:22
  78.1 2.4 %collective-permute-start.15 = (bf16[2,8,6,32,128]{4,3,2,1,0:T(8,128)(2,1)S(1)}, bf16[2,8,6,32,128]{4,3,2,1,0:T(8,128)(2,1)S(1)}, u32[]{:S(2)}, u32[]{:S(2)}) collective-permute-start(bf16[2,8,6,32,128]{4,3,2,1,0:T(8,128)(2,1)S(1)} %get-tuple-element.42.after), channel_id=1, source_target_pairs={{0,8},{8,0},{16,24},{24,16},{32,40},{40,32},{48,56},{56,48},{64,72... | collective-permute-start | bytes 2359304 | tf_op jit(solution)/shard_map/ppermute | solution.py:22
  79.0 1.7 %copy-start.7 = (f32[2,8,6,32,128]{4,3,2,1,0:T(8,128)S(1)}, f32[2,8,6,32,128]{4,3,2,1,0:T(8,128)}, u32[]{:S(2)}) copy-start(f32[2,8,6,32,128]{4,3,2,1,0:T(8,128)} %get-tuple-element.46) | copy-start | bytes 4718596
  79.0 12.1 %collective-permute-start.14 = (bf16[8,6,32,128]{3,2,1,0:T(8,128)(2,1)S(1)}, bf16[8,6,32,128]{3,2,1,0:T(8,128)(2,1)S(1)}, u32[]{:S(2)}, u32[]{:S(2)}) collective-permute-start(bf16[8,6,32,128]{3,2,1,0:T(8,128)(2,1)S(1)} %fusion.8), channel_id=1, source_target_pairs={{0,128},{8,136},{16,144},{24,152},{32,160},{40,168},{48,176},{56,1... | collective-permute-start | bytes 1179656 | tf_op jit(solution)/shard_map/ppermute | solution.py:22
  80.9 17.6 %collective-permute-start.16 = (bf16[8,6,32,128]{3,2,1,0:T(8,128)(2,1)S(1)}, bf16[8,6,32,128]{3,2,1,0:T(8,128)(2,1)S(1)}, u32[]{:S(2)}, u32[]{:S(2)}) collective-permute-start(bf16[8,6,32,128]{3,2,1,0:T(8,128)(2,1)S(1)} %fusion.9), channel_id=1, source_target_pairs={{0,128},{8,136},{16,144},{24,152},{32,160},{40,168},{48,176},{56,1... | collective-permute-start | bytes 1179656 | tf_op jit(solution)/shard_map/ppermute | solution.py:22
  90.2 8.6 %copy-start.6 = (bf16[2,1024,128]{2,1,0:T(8,128)(2,1)}, bf16[2,1024,128]{2,1,0:T(8,128)(2,1)S(1)}, u32[]{:S(2)}) copy-start(bf16[2,1024,128]{2,1,0:T(8,128)(2,1)S(1)} %get-tuple-element.52) | copy-start | bytes 1572868
  99.8 31.1 %all-to-all-start = ((bf16[8,12,32,128]{3,2,1,0:T(8,128)(2,1)}), bf16[8,12,32,128]{3,2,1,0:T(8,128)(2,1)}, u32[]{:S(2)}, u32[]{:S(2)}) async-start(bf16[8,12,32,128]{3,2,1,0:T(8,128)(2,1)} %pad_maximum_fusion), calls=%async_computation | async-start | bytes 1572864 | tf_op jit(solution)/shard_map/all_to_all | solution.py:474
  108.3 25.8 %collective-permute-start.17 = (bf16[2,1024,128]{2,1,0:T(8,128)(2,1)}, bf16[2,1024,128]{2,1,0:T(8,128)(2,1)S(1)}, u32[]{:S(2)}, u32[]{:S(2)}) collective-permute-start(bf16[2,1024,128]{2,1,0:T(8,128)(2,1)} %get-tuple-element.50), channel_id=1, source_target_pairs={{0,2},{1,3},{2,4},{3,5},{4,6},{5,7},{6,0},{7,1},{8,10},{9,11},{10,... | collective-permute-start | bytes 1572872 | tf_op jit(solution)/shard_map/ppermute | solution.py:18
  108.3 25.8 %collective-permute-start.18 = (bf16[2,1024,128]{2,1,0:T(8,128)(2,1)}, bf16[2,1024,128]{2,1,0:T(8,128)(2,1)S(1)}, u32[]{:S(2)}, u32[]{:S(2)}) collective-permute-start(bf16[2,1024,128]{2,1,0:T(8,128)(2,1)} %get-tuple-element.51), channel_id=1, source_target_pairs={{0,4},{1,5},{2,6},{3,7},{4,0},{5,1},{6,2},{7,3},{8,12},{9,13},{10,... | collective-permute-start | bytes 1572872 | tf_op jit(solution)/shard_map/ppermute | solution.py:18
  110.6 23.5 %collective-permute-start.19 = (bf16[2,1024,128]{2,1,0:T(8,128)(2,1)}, bf16[2,1024,128]{2,1,0:T(8,128)(2,1)S(1)}, u32[]{:S(2)}, u32[]{:S(2)}) collective-permute-start(bf16[2,1024,128]{2,1,0:T(8,128)(2,1)} %copy-done.6), channel_id=1, source_target_pairs={{0,6},{1,7},{2,0},{3,1},{4,2},{5,3},{6,4},{7,5},{8,14},{9,15},{10,... | collective-permute-start | bytes 1572872 | tf_op jit(solution)/shard_map/ppermute | solution.py:18
  132.1 11.0 %collective-permute-start.20 = (bf16[12,32,128]{2,1,0:T(8,128)(2,1)S(1)}, bf16[12,32,128]{2,1,0:T(8,128)(2,1)S(1)}, u32[]{:S(2)}, u32[]{:S(2)}) collective-permute-start(bf16[12,32,128]{2,1,0:T(8,128)(2,1)S(1)} %multiply_convert_fusion), channel_id=1, source_target_pairs={{1,32},{3,34},{5,36},{7,38},{9,40},{11,42},{13,44},{15,46},{17,48}... | collective-permute-start | bytes 294920 | tf_op jit(solution)/shard_map/ppermute | solution.py:488
